TPU v7x, 32 devices: a whole 2x2x4 slice. The times are simulated.
32 devices in a mesh: section: 4 (over y, x), batch: 8 (over z, core).
Axes of the slice: x: 2, y: 2, z: 4, core: 2. Of those that a mesh axis runs over, the one named last changes fastest.
Arguments:
- tokens: bfloat16 [4096, 1024], P('batch'), may hold values from -6 to 6
- cotangent: bfloat16 [4096, 1024], P('batch'), may hold values from -6 to 6
- params: bfloat16 [4, 8455168], P('section'), may hold values from -4 to 4
- lengths: int32 [8, 2, 4], P('batch'), may hold values from 1 to 160, 256 in all within a row
Outputs:
- activations: bfloat16 [4, 4096, 1024], P('section', 'batch')
- input_grads: float32 [4, 4096, 1024], P('section', 'batch')
- weight_grads: float32 [4, 8455168], P('section', 'batch')
Inputs may be any that keep to these rules, and one draw needn't show every extreme that they name: Each row of lengths sums to 256, and its largest entry is exactly 160.
All inputs are finite; a program needn't handle non-finite values.
Results may differ from a plain program's by a relative error of at most 0.02.
Values may be sent and summed in bfloat16 or wider, within the bound.
A program may use at most 448 MiB of HBM per device.

v0:
```python
import math

import jax
import jax.numpy as jnp
from jax import lax
from jax.sharding import PartitionSpec as P

D = 1024
FF = 2752
HEADS = 16
FEAT = 16
WIN = 64


EPSILON = 1e-06


def shifted(block, axis, distance):
    devices = range(lax.axis_size(axis))
    route = [(i - distance, i) for i in devices if i - distance in devices]
    return lax.ppermute(block, axis, route)


def unpack(flat, shapes):
    pieces = []
    offset = 0
    for row_count, col_count in shapes:
        pieces.append(flat[offset : offset + row_count * col_count].reshape(row_count, col_count))
        offset += row_count * col_count
    return pieces


def linear_shapes():
    return [(1, D), (D, HEADS * FEAT), (D, HEADS * FEAT), (D, D), (D, D)]


def window_shapes():
    return [(1, D), (D, D), (D, D), (D, D), (D, D)]


def feed_shapes():
    return [(1, D), (D, FF), (D, FF), (FF, D)]


def doc_masks(doc_lengths, length, window):
    positions = jnp.arange(length, dtype=jnp.int32)
    doc_ends = jnp.cumsum(doc_lengths).astype(jnp.int32)
    doc_ids = jnp.sum((positions[:, None] >= doc_ends[None, :]).astype(jnp.int32), axis=1)
    causal = positions[None, :] <= positions[:, None]
    same_doc = (doc_ids[:, None] == doc_ids[None, :]) & causal
    nearby = same_doc & (positions[:, None] - positions[None, :] < window)
    return (same_doc, nearby)


def rms_norm(values, gain_raw):
    scaled = lax.rsqrt(jnp.mean(values * values, axis=1, keepdims=True) + EPSILON)
    return values * scaled * (1.0 + gain_raw / 8.0)


def gated(gate_act, up_act):
    return jax.nn.silu(gate_act) * up_act


def plain_dot(left, right):
    return jnp.dot(left, right, preferred_element_type=jnp.float32)


def left_dot(left, right):
    return lax.dot_general(
        left, right, (((0,), (0,)), ((), ())), preferred_element_type=jnp.float32
    )


def right_dot(left, right):
    return lax.dot_general(
        left, right, (((1,), (1,)), ((), ())), preferred_element_type=jnp.float32
    )


def add_grads(total, pieces):
    offset = 0
    for piece in pieces:
        count = piece.size
        total = total.at[offset : offset + count].add(piece.reshape(-1))
        offset += count
    return total


def taylor_weights(mask):

    def weights_of(scores):
        weighted = jnp.where(mask[None], 1.0 + scores + 0.5 * scores * scores, 0.0)
        return weighted / jnp.sum(weighted, axis=2, keepdims=True)

    return weights_of


def softmax_weights(mask):

    def weights_of(scores):
        masked = jnp.where(mask[None], scores, -jnp.inf)
        top_score = jnp.max(masked, axis=2, keepdims=True)
        expo = jnp.exp(masked - top_score)
        return expo / jnp.sum(expo, axis=2, keepdims=True)

    return weights_of


def attention_pass(inputs, flat, shapes, weights_of, out_scale, grad_in, total):
    gain_raw, w_query, w_key, w_value, w_out = unpack(flat, shapes)
    length = inputs.shape[0]
    scale = 1.0 / math.sqrt(D)
    key_width = w_query.shape[1] // HEADS
    root = math.sqrt(key_width)
    values_in = inputs.astype(jnp.float32)
    normed, norm_back = jax.vjp(rms_norm, values_in, gain_raw.astype(jnp.float32))
    normed_b = normed.astype(jnp.bfloat16)
    queries = (
        (plain_dot(normed_b, w_query) * scale)
        .astype(jnp.bfloat16)
        .reshape(length, HEADS, key_width)
    )
    key_rows = (
        (plain_dot(normed_b, w_key) * scale).astype(jnp.bfloat16).reshape(length, HEADS, key_width)
    )
    value_rows = (
        (plain_dot(normed_b, w_value) * scale)
        .astype(jnp.bfloat16)
        .reshape(length, HEADS, D // HEADS)
    )
    scores = (
        jnp.einsum("ihe,jhe->hij", queries, key_rows, preferred_element_type=jnp.float32) / root
    )
    weights_f, weights_back = jax.vjp(weights_of, scores)
    weights_b = weights_f.astype(jnp.bfloat16)
    mixed = jnp.einsum("hij,jhe->ihe", weights_b, value_rows, preferred_element_type=jnp.float32)
    mixed = mixed.astype(jnp.bfloat16).reshape(length, D)
    result = values_in + plain_dot(mixed, w_out) * (out_scale * scale)
    if grad_in is None:
        return result
    grad_out_w = left_dot(mixed, grad_in) * (out_scale * scale)
    d_mixed = (right_dot(grad_in, w_out) * (out_scale * scale)).astype(jnp.bfloat16)
    d_mixed = d_mixed.reshape(length, HEADS, D // HEADS)
    d_weights = jnp.einsum("ihe,jhe->hij", d_mixed, value_rows, preferred_element_type=jnp.float32)
    d_values = jnp.einsum("hij,ihe->jhe", weights_b, d_mixed, preferred_element_type=jnp.float32)
    d_values = d_values.astype(jnp.bfloat16).reshape(length, D)
    d_scores = weights_back(d_weights)[0].astype(jnp.bfloat16)
    d_queries = (
        jnp.einsum("hij,jhe->ihe", d_scores, key_rows, preferred_element_type=jnp.float32) / root
    )
    d_queries = d_queries.astype(jnp.bfloat16).reshape(length, HEADS * key_width)
    d_keys = (
        jnp.einsum("hij,ihe->jhe", d_scores, queries, preferred_element_type=jnp.float32) / root
    )
    d_keys = d_keys.astype(jnp.bfloat16).reshape(length, HEADS * key_width)
    grad_query = left_dot(normed_b, d_queries) * scale
    grad_key = left_dot(normed_b, d_keys) * scale
    grad_value = left_dot(normed_b, d_values) * scale
    d_normed = (
        right_dot(d_queries, w_query) + right_dot(d_keys, w_key) + right_dot(d_values, w_value)
    ) * scale
    d_inputs, d_gain = norm_back(d_normed)
    d_inputs = d_inputs + grad_in.astype(jnp.float32)
    pieces = [d_gain, grad_query, grad_key, grad_value, grad_out_w]
    return (d_inputs, add_grads(total, pieces))


def feed_pass(inputs, flat, grad_in, total):
    gain_raw, w_gate, w_up, w_down = unpack(flat, feed_shapes())
    scale = 1.0 / math.sqrt(D)
    values_in = inputs.astype(jnp.float32)
    normed, norm_back = jax.vjp(rms_norm, values_in, gain_raw.astype(jnp.float32))
    normed_b = normed.astype(jnp.bfloat16)
    gate_act = plain_dot(normed_b, w_gate) * scale
    up_act = plain_dot(normed_b, w_up) * scale
    hidden_f, gated_back = jax.vjp(gated, gate_act, up_act)
    hidden = hidden_f.astype(jnp.bfloat16)
    result = values_in + plain_dot(hidden, w_down) * scale
    if grad_in is None:
        return result
    grad_down = left_dot(hidden, grad_in) * scale
    d_hidden = right_dot(grad_in, w_down) * scale
    d_gate, d_up = gated_back(d_hidden)
    d_gate = d_gate.astype(jnp.bfloat16)
    d_up = d_up.astype(jnp.bfloat16)
    grad_gate = left_dot(normed_b, d_gate) * scale
    grad_up = left_dot(normed_b, d_up) * scale
    d_normed = (right_dot(d_gate, w_gate) + right_dot(d_up, w_up)) * scale
    d_inputs, d_gain = norm_back(d_normed)
    d_inputs = d_inputs + grad_in.astype(jnp.float32)
    return (d_inputs, add_grads(total, [d_gain, grad_gate, grad_up, grad_down]))


def linear_forward(flat, inputs, doc_lengths):
    same_doc, nearby = doc_masks(doc_lengths, inputs.shape[0], WIN)
    return attention_pass(inputs, flat, linear_shapes(), taylor_weights(same_doc), 8.0, None, None)


def window_forward(flat, inputs, doc_lengths):
    same_doc, nearby = doc_masks(doc_lengths, inputs.shape[0], WIN)
    return attention_pass(inputs, flat, window_shapes(), softmax_weights(nearby), 4.0, None, None)


def feed_forward(flat, inputs, doc_lengths):
    return feed_pass(inputs, flat, None, None)


def spare_forward(flat, inputs, doc_lengths):
    return jnp.zeros(inputs.shape, jnp.float32)


def linear_backward(flat, inputs, doc_lengths, grad_in, total):
    same_doc, nearby = doc_masks(doc_lengths, inputs.shape[0], WIN)
    return attention_pass(
        inputs, flat, linear_shapes(), taylor_weights(same_doc), 8.0, grad_in, total
    )


def window_backward(flat, inputs, doc_lengths, grad_in, total):
    same_doc, nearby = doc_masks(doc_lengths, inputs.shape[0], WIN)
    return attention_pass(
        inputs, flat, window_shapes(), softmax_weights(nearby), 4.0, grad_in, total
    )


def feed_backward(flat, inputs, doc_lengths, grad_in, total):
    return feed_pass(inputs, flat, grad_in, total)


def spare_backward(flat, inputs, doc_lengths, grad_in, total):
    return (jnp.zeros(inputs.shape, jnp.float32), total)


def shards(tokens, cotangent, params, lengths):
    section_index = lax.axis_index("section")
    section_count = lax.axis_size("section")
    micro = lengths.shape[1]
    seq_rows = tokens.shape[0] // micro
    width = tokens.shape[1]
    flat = params[0]
    doc_table = lengths[0]
    token_blocks = tokens.reshape(micro, seq_rows, width)
    tangent_blocks = cotangent.reshape(micro, seq_rows, width)
    forward_fns = [linear_forward, feed_forward, window_forward, feed_forward, spare_forward]
    backward_fns = [linear_backward, feed_backward, window_backward, feed_backward, spare_backward]
    ticks = micro + section_count - 1
    received = jnp.zeros((seq_rows, width), jnp.bfloat16)
    stashed = jnp.zeros((micro, seq_rows, width), jnp.bfloat16)
    section_outs = jnp.zeros((micro, seq_rows, width), jnp.bfloat16)
    for moment in range(ticks):
        slot_index = moment - section_index
        valid = (slot_index >= 0) & (slot_index < micro)
        place = jnp.clip(slot_index, 0, micro - 1)
        inputs = jnp.where(section_index == 0, token_blocks[place], received)
        branch_pick = jnp.where(valid, section_index, section_count)
        result = lax.switch(branch_pick, forward_fns, flat, inputs, doc_table[place])
        result_b = result.astype(jnp.bfloat16)
        stashed = stashed.at[place].set(jnp.where(valid, inputs, stashed[place]))
        section_outs = section_outs.at[place].set(jnp.where(valid, result_b, section_outs[place]))
        if moment < ticks - 1:
            received = shifted(result_b, "section", 1)
    received = jnp.zeros((seq_rows, width), jnp.bfloat16)
    grad_total = jnp.zeros(flat.shape, jnp.float32)
    grads_in = jnp.zeros((micro, seq_rows, width), jnp.float32)
    for moment in range(ticks):
        slot_index = micro - 1 - moment + (section_count - 1 - section_index)
        valid = (slot_index >= 0) & (slot_index < micro)
        place = jnp.clip(slot_index, 0, micro - 1)
        incoming = jnp.where(section_index == section_count - 1, tangent_blocks[place], received)
        branch_pick = jnp.where(valid, section_index, section_count)
        d_inputs, grad_total = lax.switch(
            branch_pick, backward_fns, flat, stashed[place], doc_table[place], incoming, grad_total
        )
        grads_in = grads_in.at[place].set(jnp.where(valid, d_inputs, grads_in[place]))
        if moment < ticks - 1:
            received = shifted(d_inputs.astype(jnp.bfloat16), "section", -1)
    final_sum = lax.psum_scatter(grad_total, "batch", scatter_dimension=0, tiled=True)
    activations = section_outs.reshape(1, micro * seq_rows, width)
    input_grads = grads_in.reshape(1, micro * seq_rows, width)
    return (activations, input_grads, final_sum[None])


def solution(mesh):
    return jax.shard_map(
        shards,
        mesh=mesh,
        in_specs=(P("batch", None), P("batch", None), P("section", None), P("batch", None, None)),
        out_specs=(P("section", "batch", None), P("section", "batch", None), P("section", "batch")),
        check_vma=False,
    )
```

profile of v0, /device:TPU:8, one launch (start us, length us, event | category | flops | bytes accessed | tf_op | source)
XLA Modules:
  0.0 2309.9 jit_solution(6223907760672141392)
XLA Ops:
  7.3 357.8 %reduce.235 = bf16[8455168]{0:T(1024)(128)(2,1)} reduce(bf16[1,8455168]{1,0:T(2,128)(2,1)} %param.266, bf16[]{:T(256)} %constant.3528), dimensions={0}, to_apply=%param.266.reduce_sub_computation | reduce | bytes 33820672 | tf_op args[2]
  367.5 48.9 %conditional.10 = (bf16[256,1024]{1,0:T(8,128)(2,1)S(1)}) conditional(s32[]{:T(128)} %clamp.20, (bf16[256,1024]{1,0:T(8,128)(2,1)S(1)}, bf16[8455168]{0:T(1024)(128)(2,1)}, s32[4]{0:T(128)}) %tuple.650, (bf16[256,1024]{1,0:T(8,128)(2,1)S(1)}, bf16[8455168]{0:T(1024)(128)(2,1)}) %tuple.651, ...), branch_computations={%region_1.6_spmd, %region_6.8_spmd, %region_8.14_spmd, %region_14.... | conditional | flops 4338093056 | bytes 92294152 | solution.py:256
  418.7 10.5 collective-permute-done
  431.0 48.5 %conditional.11 = (bf16[256,1024]{1,0:T(8,128)(2,1)S(1)}) conditional(s32[]{:T(128)} %clamp.21, (bf16[256,1024]{1,0:T(8,128)(2,1)S(1)}, bf16[8455168]{0:T(1024)(128)(2,1)}, s32[4]{0:T(128)S(1)}) %tuple.653, (bf16[256,1024]{1,0:T(8,128)(2,1)S(1)}, bf16[8455168]{0:T(1024)(128)(2,1)}) %tuple.654, ...), branch_computations={%region_18.23_spmd, %region_23.25_spmd, %region_25.31_spmd, %regio... | conditional | flops 4338093056 | bytes 92294152 | solution.py:256
  479.6 32.6 %collective-permute-start.1 = (bf16[256,1024]{1,0:T(8,128)(2,1)S(1)}, bf16[256,1024]{1,0:T(8,128)(2,1)S(1)}, u32[]{:S(2)}, u32[]{:S(2)}) collective-permute-start(bf16[256,1024]{1,0:T(8,128)(2,1)S(1)} %get-tuple-element.2164), channel_id=1, source_target_pairs={{0,8},{8,16},{16,24},{1,9},{9,17},{17,25},{2,10},{10,18},{18,26},{... | collective-permute-start | bytes 1572872 | tf_op jit(solution)/shard_map/ppermute | solution.py:21
  523.8 18.1 conditional.12
  541.9 62.9 %collective-permute-start.2 = (bf16[256,1024]{1,0:T(8,128)(2,1)}, bf16[256,1024]{1,0:T(8,128)(2,1)S(1)}, u32[]{:S(2)}, u32[]{:S(2)}) collective-permute-start(bf16[256,1024]{1,0:T(8,128)(2,1)} %get-tuple-element.2165), channel_id=1, source_target_pairs={{0,8},{8,16},{16,24},{1,9},{9,17},{17,25},{2,10},{10,18},{18,26},{... | collective-permute-start | bytes 1572872 | tf_op jit(solution)/shard_map/ppermute | solution.py:21
  615.7 19.3 conditional.13
  651.4 42.5 %conditional.15 = (f32[256,1024]{1,0:T(8,128)S(1)}, f32[8455168]{0:T(1024)}) conditional(s32[]{:T(128)} %clamp.24, (bf16[256,1024]{1,0:T(8,128)(2,1)S(1)}, bf16[8455168]{0:T(1024)(128)(2,1)}, s32[4]{0:T(128)S(1)}, bf16[256,1024]{1,0:T(8,128)(2,1)S(1)}) %tuple.986, (bf16[8455168]{0:T(1024)(128)(2,1)}, ...), branch_computations={%region_85.0_spmd, %region_93.97_spmd, %region_97.0_spmd, %region_... | conditional | flops 11582461952 | bytes 572133760 | solution.py:271
  682.6 11.1 broadcast_in_dim.386
  695.3 43.9 %collective-permute-done.4 = bf16[256,1024]{1,0:T(8,128)(2,1)S(1)} collective-permute-done((bf16[256,1024]{1,0:T(8,128)(2,1)S(1)}, bf16[256,1024]{1,0:T(8,128)(2,1)S(1)}, u32[]{:S(2)}, u32[]{:S(2)}) %collective-permute-start.4) | collective-permute-done | bytes 524320 | tf_op jit(solution)/shard_map/ppermute | solution.py:21
  740.4 56.4 %conditional.16 = (f32[256,1024]{1,0:T(8,128)S(1)}, f32[8455168]{0:T(1024)}) conditional(s32[]{:T(128)} %clamp.23, (bf16[256,1024]{1,0:T(8,128)(2,1)S(1)}, bf16[8455168]{0:T(1024)(128)(2,1)}, s32[4]{0:T(128)S(1)}, bf16[256,1024]{1,0:T(8,128)(2,1)S(1)}, f32[8455168]{0:T(1024)}) %tuple.998, ...), branch_computations={%region_113.121_spmd, %region_121.125_spmd, %region_125.0_spmd, %r... | conditional | flops 11585280000 | bytes 532685056 | solution.py:271
  771.6 24.8 %copy.738 = f32[8455168]{0:T(1024)} copy(f32[8455168]{0:T(1024)} %param.244) | data formatting | bytes 67641344 | tf_op jit(solution)/shard_map/cond
  798.1 15.9 collective-permute-done.5
  815.2 37.1 %conditional.17 = (f32[256,1024]{1,0:T(8,128)S(1)}, f32[8455168]{0:T(1024)}) conditional(s32[]{:T(128)} %clamp.22, (bf16[256,1024]{1,0:T(8,128)(2,1)S(1)}, bf16[8455168]{0:T(1024)(128)(2,1)}, s32[4]{0:T(128)S(1)}, bf16[256,1024]{1,0:T(8,128)(2,1)S(1)}, f32[8455168]{0:T(1024)}) %tuple.994, ...), branch_computations={%region_141.149_spmd, %region_149.153_spmd, %region_153.164_spmd, ... | conditional | flops 11585280000 | bytes 465043712 | solution.py:271
  853.6 427.7 %collective-permute-done.6 = bf16[256,1024]{1,0:T(8,128)(2,1)S(1)} collective-permute-done((bf16[256,1024]{1,0:T(8,128)(2,1)S(1)}, bf16[256,1024]{1,0:T(8,128)(2,1)S(1)}, u32[]{:S(2)}, u32[]{:S(2)}) %collective-permute-start.6) | collective-permute-done | bytes 524320 | tf_op jit(solution)/shard_map/ppermute | solution.py:21
  1282.5 112.6 %conditional.18 = (f32[256,1024]{1,0:T(8,128)S(1)}, f32[8455168]{0:T(1024)}) conditional(s32[]{:T(128)} %clamp.21, (bf16[256,1024]{1,0:T(8,128)(2,1)S(1)}, bf16[8455168]{0:T(1024)(128)(2,1)}, s32[4]{0:T(128)S(1)}, bf16[256,1024]{1,0:T(8,128)(2,1)S(1)}, f32[8455168]{0:T(1024)}) %tuple.990, ...), branch_computations={%region_169.177_spmd, %region_177.181_spmd, %region_181.192_spmd, ... | conditional | flops 11585280000 | bytes 532685056 | solution.py:271
  1338.1 24.8 %copy.752 = f32[8455168]{0:T(1024)} copy(f32[8455168]{0:T(1024)} %fusion.679) | data formatting | bytes 67641344 | tf_op jit(solution)/shard_map/cond
  1396.4 134.1 %collective-permute-done.7 = bf16[256,1024]{1,0:T(8,128)(2,1)S(1)} collective-permute-done((bf16[256,1024]{1,0:T(8,128)(2,1)S(1)}, bf16[256,1024]{1,0:T(8,128)(2,1)S(1)}, u32[]{:S(2)}, u32[]{:S(2)}) %collective-permute-start.7) | collective-permute-done | bytes 524320 | tf_op jit(solution)/shard_map/ppermute | solution.py:21
  1531.6 93.3 %conditional.19 = (f32[256,1024]{1,0:T(8,128)S(1)}, f32[8455168]{0:T(1024)}) conditional(s32[]{:T(128)} %clamp.20, (bf16[256,1024]{1,0:T(8,128)(2,1)S(1)}, bf16[8455168]{0:T(1024)(128)(2,1)}, s32[4]{0:T(128)}, bf16[256,1024]{1,0:T(8,128)(2,1)S(1)}, f32[8455168]{0:T(1024)}) %tuple.962, (bf16[8455168]{0:T(1024)(128)(2,1)}, ...), branch_computations={%region_197.205_spmd, %region_205.209_spmd, %region_209.220_spmd, ... | conditional | flops 11585280000 | bytes 459407616 | solution.py:271
  1583.1 4.8 fusion.782
  1627.2 21.6 conditional.14
  1656.8 622.3 %all-reduce.7.cloned.1.call-done = f32[8455168]{0:T(1024)} async-done(((f32[8455168]{0:T(1024)}), f32[8455168]{0:T(1024)}) %all-reduce.7.cloned.1.call-update) | async-done | bytes 33820688
  2282.0 20.6 broadcast_in_dim.479
  (280 shorter events, 242.9 us)
Async XLA Ops:
  7.2 2271.9 %all-reduce.7.cloned.1.call-start = ((), (), s32[]{:S(2)}) async-start(), calls=%async_computation | async-start | bytes 67641344
  7.2 357.8 %copy-start.89 = (s32[3]{0:T(128)S(1)}, s32[3]{0:T(128)}, u32[]{:S(2)}) copy-start(s32[3]{0:T(128)} %constant.3508.clone.1) | copy-start | bytes 40
  7.3 358.7 %copy-start.40 = (bf16[512,1024]{1,0:T(8,128)(2,1)S(1)}, bf16[512,1024]{1,0:T(8,128)(2,1)}, u32[]{:S(2)}) copy-start(bf16[512,1024]{1,0:T(8,128)(2,1)} %param.264) | copy-start | bytes 3145732
  7.3 359.6 %copy-start.88 = (s32[1,2,4]{2,1,0:T(2,128)S(1)}, s32[1,2,4]{2,1,0:T(2,128)}, u32[]{:S(2)}) copy-start(s32[1,2,4]{2,1,0:T(2,128)} %param.267) | copy-start | bytes 100
  367.5 63.5 %copy-start.92 = (s32[4]{0:T(128)}, s32[4]{0:T(128)S(1)}, u32[]{:S(2)}) copy-start(s32[4]{0:T(128)S(1)} %get-tuple-element.2106) | copy-start | bytes 52
  416.4 12.7 collective-permute-start
  479.6 43.2 %collective-permute-start.1 = (bf16[256,1024]{1,0:T(8,128)(2,1)S(1)}, bf16[256,1024]{1,0:T(8,128)(2,1)S(1)}, u32[]{:S(2)}, u32[]{:S(2)}) collective-permute-start(bf16[256,1024]{1,0:T(8,128)(2,1)S(1)} %get-tuple-element.2164), channel_id=1, source_target_pairs={{0,8},{8,16},{16,24},{1,9},{9,17},{17,25},{2,10},{10,18},{18,26},{... | collective-permute-start | bytes 1572872 | tf_op jit(solution)/shard_map/ppermute | solution.py:21
  541.9 73.8 %copy-start.96 = (s32[4]{0:T(128)S(1)}, s32[4]{0:T(128)}, u32[]{:S(2)}) copy-start(s32[4]{0:T(128)} %get-tuple-element.2108) | copy-start | bytes 52
  541.9 72.8 %collective-permute-start.2 = (bf16[256,1024]{1,0:T(8,128)(2,1)}, bf16[256,1024]{1,0:T(8,128)(2,1)S(1)}, u32[]{:S(2)}, u32[]{:S(2)}) collective-permute-start(bf16[256,1024]{1,0:T(8,128)(2,1)} %get-tuple-element.2165), channel_id=1, source_target_pairs={{0,8},{8,16},{16,24},{1,9},{9,17},{17,25},{2,10},{10,18},{18,26},{... | collective-permute-start | bytes 1572872 | tf_op jit(solution)/shard_map/ppermute | solution.py:21
  635.1 13.2 collective-permute-start.3
  651.4 88.9 %copy-start.3 = (bf16[256,1024]{1,0:T(8,128)(2,1)S(1)}, bf16[256,1024]{1,0:T(8,128)(2,1)}, u32[]{:S(2)}) copy-start(bf16[256,1024]{1,0:T(8,128)(2,1)} %get-tuple-element.2100) | copy-start | bytes 1572868
  651.4 88.9 %copy-start.97 = (s32[4]{0:T(128)S(1)}, s32[4]{0:T(128)}, u32[]{:S(2)}) copy-start(s32[4]{0:T(128)} %get-tuple-element.2108) | copy-start | bytes 52
  694.0 45.2 %collective-permute-start.4 = (bf16[256,1024]{1,0:T(8,128)(2,1)S(1)}, bf16[256,1024]{1,0:T(8,128)(2,1)S(1)}, u32[]{:S(2)}, u32[]{:S(2)}) collective-permute-start(bf16[256,1024]{1,0:T(8,128)(2,1)S(1)} %convert_element_type.1342), channel_id=1, source_target_pairs={{8,0},{16,8},{24,16},{9,1},{17,9},{25,17},{10,2},{18,10},{26,18},{... | collective-permute-start | bytes 1572872 | tf_op jit(solution)/shard_map/ppermute | solution.py:21
  740.4 74.8 %copy-start.2 = (bf16[256,1024]{1,0:T(8,128)(2,1)S(1)}, bf16[256,1024]{1,0:T(8,128)(2,1)}, u32[]{:S(2)}) copy-start(bf16[256,1024]{1,0:T(8,128)(2,1)} %get-tuple-element.2099) | copy-start | bytes 1572868
  740.4 74.8 %copy-start.95 = (s32[4]{0:T(128)S(1)}, s32[4]{0:T(128)}, u32[]{:S(2)}) copy-start(s32[4]{0:T(128)} %get-tuple-element.2105) | copy-start | bytes 52
  796.8 17.2 collective-permute-start.5
  815.1 467.3 %copy-start.1 = (bf16[256,1024]{1,0:T(8,128)(2,1)S(1)}, bf16[256,1024]{1,0:T(8,128)(2,1)}, u32[]{:S(2)}) copy-start(bf16[256,1024]{1,0:T(8,128)(2,1)} %get-tuple-element.2098) | copy-start | bytes 1572868
  815.1 467.3 %copy-start.93 = (s32[4]{0:T(128)S(1)}, s32[4]{0:T(128)}, u32[]{:S(2)}) copy-start(s32[4]{0:T(128)} %copy-done.92) | copy-start | bytes 52
  852.2 430.2 %copy-start.15 = (f32[256,1024]{1,0:T(8,128)}, f32[256,1024]{1,0:T(8,128)S(1)}, u32[]{:S(2)}) copy-start(f32[256,1024]{1,0:T(8,128)S(1)} %get-tuple-element.1724) | copy-start | bytes 3145732
  852.3 429.0 %collective-permute-start.6 = (bf16[256,1024]{1,0:T(8,128)(2,1)S(1)}, bf16[256,1024]{1,0:T(8,128)(2,1)S(1)}, u32[]{:S(2)}, u32[]{:S(2)}) collective-permute-start(bf16[256,1024]{1,0:T(8,128)(2,1)S(1)} %convert_element_type.1344), channel_id=1, source_target_pairs={{8,0},{16,8},{24,16},{9,1},{17,9},{25,17},{10,2},{18,10},{26,18},{... | collective-permute-start | bytes 1572872 | tf_op jit(solution)/shard_map/ppermute | solution.py:21
  1282.4 249.2 %copy-start = (bf16[256,1024]{1,0:T(8,128)(2,1)S(1)}, bf16[256,1024]{1,0:T(8,128)(2,1)}, u32[]{:S(2)}) copy-start(bf16[256,1024]{1,0:T(8,128)(2,1)} %get-tuple-element.2097) | copy-start | bytes 1572868
  1395.0 136.6 %copy-start.13 = (f32[256,1024]{1,0:T(8,128)}, f32[256,1024]{1,0:T(8,128)S(1)}, u32[]{:S(2)}) copy-start(f32[256,1024]{1,0:T(8,128)S(1)} %get-tuple-element.1726) | copy-start | bytes 3145732
  1395.1 135.4 %collective-permute-start.7 = (bf16[256,1024]{1,0:T(8,128)(2,1)S(1)}, bf16[256,1024]{1,0:T(8,128)(2,1)S(1)}, u32[]{:S(2)}, u32[]{:S(2)}) collective-permute-start(bf16[256,1024]{1,0:T(8,128)(2,1)S(1)} %convert_element_type.1345), channel_id=1, source_target_pairs={{8,0},{16,8},{24,16},{9,1},{17,9},{25,17},{10,2},{18,10},{26,18},{... | collective-permute-start | bytes 1572872 | tf_op jit(solution)/shard_map/ppermute | solution.py:21
  1656.8 625.1 %copy-start.8 = (f32[2,256,1024]{2,1,0:T(8,128)}, f32[2,256,1024]{2,1,0:T(8,128)S(1)}, u32[]{:S(2)}) copy-start(f32[2,256,1024]{2,1,0:T(8,128)S(1)} %fusion.881) | copy-start | bytes 6291460
  (31 other events, 174.1 us)
Sparse Core Ops, SparseCore 0:
  1625.1 653.9 all-reduce.6
where the time goes:
time: 2330 us; the launch traced here: 2310 us
  waiting for transfers between devices  1270 us (55%)
  other arithmetic  429 us (18%)
  loops' own time  257 us (11%)
  local copies, waits for them, and re-layouts  182 us (8%)
  starting transfers between devices  107 us (5%)
  matrix products  52.1 us (2%)
    ppermute x8, waiting for transfers between devices, shifted(): return lax.ppermute(block, axis, route)  644 us
    unnamed x2, waiting for transfers between devices  622 us
    unnamed x1, other arithmetic  358 us
    another operation x5, loops' own time, shards(): lax.switch(branch_pick, backward_fns, flat, stashed[place], doc_table[pla...  163 us
    ppermute x8, starting transfers between devices, shifted(): return lax.ppermute(block, axis, route)  106 us
    another operation x5, loops' own time, shards(): lax.switch(branch_pick, forward_fns, flat, inputs, doc_table[place])  94.4 us
    slice x24, local copies, waits for them, and re-layouts, unpack(): flat[offset:offset + row_count * col_count].reshape(row_count, col_count)  69.1 us
    cond x32, local copies, waits for them, and re-layouts  56.3 us
  transfers between devices with their start and end apart: 9, of which 9 were waited for; matrix products, arithmetic and copies ran while one was open for 1% of the time, Pallas kernels for 0%

commit v1 on v0

v1 whole, which is shorter than its diff:
```python
import functools
import math

import jax
import jax.numpy as jnp
from jax import lax
from jax.experimental import pallas as pl
from jax.experimental.pallas import tpu as pltpu
from jax.sharding import PartitionSpec as P

D = 1024
FF = 2752
FP = 2816
HEADS = 16
FEAT = 16
WIN = 64
MICRO = 2
LEN = 256
EPSILON = 1e-06
SCALE = 1.0 / math.sqrt(D)
LINEAR, FEED, WINDOW, FEED2 = 0, 1, 2, 3
MIB = 2**20
MESH = pl.DeviceIdType.MESH
BF = jnp.bfloat16
F32 = jnp.float32


def any_spec():
    return pl.BlockSpec(memory_space=pl.ANY)


def vmem_spec():
    return pl.BlockSpec(memory_space=pltpu.VMEM)


def dot(left, right):
    return jnp.dot(left, right, preferred_element_type=F32)


def dot_t(left, right):
    return lax.dot_general(left, right, (((1,), (1,)), ((), ())), preferred_element_type=F32)


def dot_0(left, right):
    return lax.dot_general(left, right, (((0,), (0,)), ((), ())), preferred_element_type=F32)


def at256(index):
    return pl.ds(pl.multiple_of(index * 256, 256), 256)


def is_feed(section):
    return (section == FEED) | (section == FEED2)


PAIR_STEP = 32 * FF
ROW_STEP = 64 * D


def prepare_kernel(flat, wide, tall, chunk, blocks, woven, stage_pair, stage_row, stage_low, load_sem, store_sem):
    section = lax.axis_index("section")

    def run(steps, count, source, target, stage, work):
        def load(i, slot):
            return pltpu.make_async_copy(
                flat.at[:, pl.ds(pl.multiple_of(source(i), 1024), count)],
                chunk.at[slot, :, pl.ds(0, count)],
                load_sem.at[slot],
            )

        def store(i, slot):
            return pltpu.make_async_copy(stage.at[slot], target(i), store_sem.at[slot])

        load(0, 0).start()

        def step(i, carry):
            slot = lax.rem(i, 2)

            @pl.when(i + 1 < steps)
            def _():
                load(i + 1, 1 - slot).start()

            load(i, slot).wait()

            @pl.when(i >= 2)
            def _():
                store(i - 2, slot).wait()

            rows = count // 128
            blocks[pl.ds(0, rows), :] = chunk[slot, :, pl.ds(0, count)].astype(F32).reshape(rows, 128)
            work(slot)
            store(i, slot).start()
            return carry

        lax.fori_loop(0, steps, step, 0)
        store(steps - 2, steps % 2).wait()
        store(steps - 1, (steps - 1) % 2).wait()

    def pair_work(slot):
        low_half = lax.broadcasted_iota(jnp.int32, (16, 128), 1) < 64
        rolled = None
        for c in range(22):
            even = blocks[pl.ds(c, 16, stride=43), :]
            if c == 21:
                even = jnp.where(low_half, even, 0.0)
            if rolled is None:
                rolled = pltpu.roll(blocks[pl.ds(21, 16, stride=43), :], 64, 1)
            if c < 21:
                after = pltpu.roll(blocks[pl.ds(22 + c, 16, stride=43), :], 64, 1)
                odd = jnp.where(low_half, rolled, after)
                rolled = after
            else:
                odd = jnp.where(low_half, rolled, 0.0)
            woven[c, pl.ds(0, 16, stride=2), :] = even
            woven[c, pl.ds(1, 16, stride=2), :] = odd
        for c in range(22):
            stage_pair[slot, :, pl.ds(128 * c, 128)] = woven[c].astype(BF)

    def row_work(slot):
        for c in range(8):
            stage_row[slot, :, pl.ds(128 * c, 128)] = blocks[pl.ds(c, 64, stride=8), :].astype(BF)

    def low_work(slot):
        for c in range(2):
            stage_low[slot, :, pl.ds(128 * c, 128)] = blocks[pl.ds(c, 256, stride=2), :].astype(BF)

    def rows_of(index, count):
        return pl.ds(pl.multiple_of(index * count, count), count)

    def square(first, target):
        run(16, ROW_STEP, lambda i: D + first + i * ROW_STEP, target, stage_row, row_work)

    @pl.when(is_feed(section))
    def _():
        run(
            64,
            PAIR_STEP,
            lambda i: D + i * PAIR_STEP,
            lambda i: wide.at[i // 32, rows_of(lax.rem(i, 32), 32), :],
            stage_pair,
            pair_work,
        )
        run(
            43,
            ROW_STEP,
            lambda i: D + 2 * D * FF + i * ROW_STEP,
            lambda i: tall.at[rows_of(i, 64), :],
            stage_row,
            row_work,
        )
        stage_row[0] = jnp.zeros((64, D), BF)
        last = pltpu.make_async_copy(stage_row.at[0], tall.at[pl.ds(FF, 64), :], store_sem.at[0])
        last.start()
        last.wait()

    @pl.when(section == WINDOW)
    def _():
        square(0, lambda i: wide.at[0, rows_of(i, 64), pl.ds(0, D)])
        square(D * D, lambda i: wide.at[0, rows_of(i, 64), pl.ds(D, D)])
        square(2 * D * D, lambda i: wide.at[1, rows_of(i, 64), pl.ds(0, D)])
        square(3 * D * D, lambda i: tall.at[rows_of(i, 64), :])

    @pl.when(section == LINEAR)
    def _():
        width = HEADS * FEAT
        for part in range(2):
            run(
                4,
                ROW_STEP,
                lambda i, part=part: D + part * D * width + i * ROW_STEP,
                lambda i, part=part: wide.at[0, rows_of(i, 256), pl.ds(part * width, width)],
                stage_low,
                low_work,
            )
        square(2 * D * width, lambda i: wide.at[1, rows_of(i, 64), pl.ds(0, D)])
        square(2 * D * width + D * D, lambda i: tall.at[rows_of(i, 64), :])


def prepare(flat):
    return pl.pallas_call(
        prepare_kernel,
        out_shape=(jax.ShapeDtypeStruct((2, D, FP), BF), jax.ShapeDtypeStruct((FP, D), BF)),
        in_specs=[any_spec()],
        out_specs=(any_spec(), any_spec()),
        scratch_shapes=[
            pltpu.VMEM((2, 1, PAIR_STEP), BF),
            pltpu.VMEM((PAIR_STEP // 128, 128), F32),
            pltpu.VMEM((22, 32, 128), F32),
            pltpu.VMEM((2, 32, FP), BF),
            pltpu.VMEM((2, 64, D), BF),
            pltpu.VMEM((2, 256, 256), BF),
            pltpu.SemaphoreType.DMA((2,)),
            pltpu.SemaphoreType.DMA((2,)),
        ],
        compiler_params=pltpu.CompilerParams(vmem_limit_bytes=32 * MIB),
        name="prepare",
    )(flat)


def lane_of_head(section_kind, block, half):
    lanes = lax.broadcasted_iota(jnp.int32, (1, 128), 1)
    if section_kind == WINDOW:
        return lanes // 64 == half
    return lanes // FEAT == lax.rem(2 * block + half, 8)


def lane_of_value(half):
    return lax.broadcasted_iota(jnp.int32, (1, 128), 1) // 64 == half


def only(mask, values):
    return jnp.where(mask, values, jnp.zeros_like(values))


def query_block(section_kind, block):
    index = block if section_kind == WINDOW else block // 4
    return pl.ds(pl.multiple_of(index * 128, 128), 128)


def key_block(section_kind, block):
    first = D if section_kind == WINDOW else HEADS * FEAT
    index = block if section_kind == WINDOW else block // 4
    return pl.ds(pl.multiple_of(first + index * 128, 128), 128)


def value_block(block, first=0):
    return pl.ds(pl.multiple_of(first + block * 128, 128), 128)


def mask_of(section_kind, doc_col, doc_row):
    rows = lax.broadcasted_iota(jnp.int32, (LEN, LEN), 0)
    cols = lax.broadcasted_iota(jnp.int32, (LEN, LEN), 1)
    mask = (doc_col == doc_row) & (cols <= rows)
    if section_kind == WINDOW:
        mask = mask & (rows - cols < WIN)
    return mask.astype(F32)


def root_of(section_kind):
    return 1.0 / math.sqrt(D // HEADS if section_kind == WINDOW else FEAT)


def weigh(section_kind, scores, mask):
    if section_kind == WINDOW:
        kept = jnp.where(mask > 0.0, scores, -1e30)
        raised = jnp.exp(kept - jnp.max(kept, axis=1, keepdims=True))
        raised = raised * mask
        inverse = 1.0 / jnp.sum(raised, axis=1, keepdims=True)
        return raised * inverse, inverse
    raised = mask * (1.0 + scores + 0.5 * scores * scores)
    inverse = 1.0 / jnp.sum(raised, axis=1, keepdims=True)
    return raised * inverse, inverse


def unweigh(section_kind, scores, mask, weights, inverse, d_weights):
    centred = d_weights - jnp.sum(d_weights * weights, axis=1, keepdims=True)
    if section_kind == WINDOW:
        return weights * centred
    return centred * inverse * (mask * (1.0 + scores))


def out_scale(section_kind):
    return {LINEAR: 8.0, WINDOW: 4.0, FEED: 1.0}[section_kind] * SCALE


def load_weights(section, wide, tall, wide_v, tall_v, sems):
    def copies(kind):
        if kind == FEED:
            return [
                pltpu.make_async_copy(wide, wide_v, sems.at[0]),
                pltpu.make_async_copy(tall, tall_v, sems.at[1]),
            ]
        first = 2 * D if kind == WINDOW else 2 * HEADS * FEAT
        return [
            pltpu.make_async_copy(wide.at[0, :, pl.ds(0, first)], wide_v.at[0, :, pl.ds(0, first)], sems.at[0]),
            pltpu.make_async_copy(wide.at[1, :, pl.ds(0, D)], wide_v.at[1, :, pl.ds(0, D)], sems.at[1]),
            pltpu.make_async_copy(tall.at[pl.ds(0, D), :], tall_v.at[pl.ds(0, D), :], sems.at[2]),
        ]

    def each(act):
        for kind, here in ((FEED, is_feed(section)), (WINDOW, section == WINDOW), (LINEAR, section == LINEAR)):

            @pl.when(here)
            def _(kind=kind):
                for copy in copies(kind):
                    act(copy)

    each(lambda copy: copy.start())
    return lambda: each(lambda copy: copy.wait())


def forward_kernel(
    tokens, flat, wide, tall, doc_col, doc_row,
    acts, inputs, normed, first, second,
    wide_v, tall_v, gain_v, z_v, h_v, x_v, first_v, second_v, mid_v, mask_v,
    weight_sem, gain_sem, in_sem, out_sem, send_sem, recv_sem,
):
    section = lax.axis_index("section")
    batch = lax.axis_index("batch")
    last = lax.axis_size("section") - 1
    barrier = pltpu.get_barrier_semaphore()

    @pl.when(section > 0)
    def _():
        pl.semaphore_signal(barrier, inc=1, device_id=(section - 1, batch), device_id_type=MESH)

    @pl.when(section < last)
    def _():
        pl.semaphore_signal(barrier, inc=1, device_id=(section + 1, batch), device_id_type=MESH)

    gain_copy = pltpu.make_async_copy(flat.at[:, pl.ds(0, D)], gain_v, gain_sem)
    gain_copy.start()
    wait_weights = load_weights(section, wide, tall, wide_v, tall_v, weight_sem)

    def rows_at(micro):
        return pl.ds(micro * LEN, LEN)

    def token_copy(micro):
        return pltpu.make_async_copy(tokens.at[rows_at(micro), :], z_v.at[micro], in_sem.at[micro])

    @pl.when(section == 0)
    def _():
        for micro in range(MICRO):
            token_copy(micro).start()

    pl.semaphore_wait(barrier, jnp.where((section > 0) & (section < last), 2, 1))
    gain_copy.wait()
    wait_weights()
    gain = 1.0 + gain_v[...].astype(F32) / 8.0

    def hand_on(micro):
        return pltpu.make_async_remote_copy(
            src_ref=x_v.at[micro],
            dst_ref=z_v.at[micro],
            send_sem=send_sem.at[micro],
            recv_sem=recv_sem.at[micro],
            device_id=(section + 1, batch),
            device_id_type=MESH,
        )

    def norm(micro):
        z = z_v[micro].astype(F32)
        scaled = lax.rsqrt(jnp.mean(z * z, axis=1, keepdims=True) + EPSILON)
        h_v[micro] = (z * scaled * gain).astype(BF)

    def finish(micro, source, depth, scale):
        def tile(n, carry):
            cols = at256(n)
            branch = dot(source[:, pl.ds(0, depth)], tall_v[pl.ds(0, depth), cols]) * scale
            x_v[micro, :, cols] = (z_v[micro, :, cols].astype(F32) + branch).astype(BF)
            return carry

        lax.fori_loop(0, D // 256, tile, 0)

    def feed(micro):
        def tile(t, carry):
            cols = at256(t)
            gate = dot(h_v[micro], wide_v[0, :, cols]) * SCALE
            up = dot(h_v[micro], wide_v[1, :, cols]) * SCALE
            first_v[micro, :, cols] = gate.astype(BF)
            second_v[micro, :, cols] = up.astype(BF)
            mid_v[:, cols] = (gate / (1.0 + jnp.exp(-gate)) * up).astype(BF)
            return carry

        lax.fori_loop(0, FP // 256, tile, 0)
        finish(micro, mid_v, FP, SCALE)

    def attend(micro, kind):
        def project(which, count, target):
            def tile(t, carry):
                cols = at256(t)
                target[micro, :, cols] = (dot(h_v[micro], wide_v[which, :, cols]) * SCALE).astype(BF)
                return carry

            lax.fori_loop(0, count, tile, 0)

        project(0, 8 if kind == WINDOW else 2, first_v)
        project(1, 4, second_v)
        mask_v[...] = mask_of(kind, doc_col[micro], doc_row[micro])

        def block(t, carry):
            queries = first_v[micro, :, query_block(kind, t)]
            keys = first_v[micro, :, key_block(kind, t)]
            values = second_v[micro, :, value_block(t)]
            mixed = jnp.zeros((LEN, 128), F32)
            for half in range(2):
                scores = dot_t(only(lane_of_head(kind, t, half), queries), keys) * root_of(kind)
                weights, _ = weigh(kind, scores, mask_v[...])
                mixed += dot(weights.astype(BF), only(lane_of_value(half), values))
            second_v[micro, :, value_block(t, D)] = mixed.astype(BF)
            mid_v[:, value_block(t)] = mixed.astype(BF)
            return carry

        lax.fori_loop(0, 8, block, 0)
        finish(micro, mid_v, D, out_scale(kind))

    def outs(micro):
        rows = rows_at(micro)
        return [
            pltpu.make_async_copy(x_v.at[micro], acts.at[rows, :], out_sem.at[micro, 0]),
            pltpu.make_async_copy(z_v.at[micro], inputs.at[rows, :], out_sem.at[micro, 1]),
            pltpu.make_async_copy(h_v.at[micro], normed.at[rows, :], out_sem.at[micro, 2]),
            pltpu.make_async_copy(first_v.at[micro], first.at[rows, :], out_sem.at[micro, 3]),
            pltpu.make_async_copy(second_v.at[micro], second.at[rows, :], out_sem.at[micro, 4]),
        ]

    for micro in range(MICRO):

        @pl.when(section == 0)
        def _(micro=micro):
            token_copy(micro).wait()

        @pl.when(section > 0)
        def _(micro=micro):
            hand_on(micro).wait_recv()

        norm(micro)

        @pl.when(is_feed(section))
        def _(micro=micro):
            feed(micro)

        @pl.when(section == WINDOW)
        def _(micro=micro):
            attend(micro, WINDOW)

        @pl.when(section == LINEAR)
        def _(micro=micro):
            attend(micro, LINEAR)

        @pl.when(section < last)
        def _(micro=micro):
            hand_on(micro).start()

        for copy in outs(micro):
            copy.start()

    for micro in range(MICRO):

        @pl.when(section < last)
        def _(micro=micro):
            hand_on(micro).wait_send()

        for copy in outs(micro):
            copy.wait()


def forward(tokens, flat, wide, tall, doc_col, doc_row):
    count = MICRO * LEN
    return pl.pallas_call(
        forward_kernel,
        out_shape=(
            jax.ShapeDtypeStruct((count, D), BF),
            jax.ShapeDtypeStruct((count, D), BF),
            jax.ShapeDtypeStruct((count, D), BF),
            jax.ShapeDtypeStruct((count, FP), BF),
            jax.ShapeDtypeStruct((count, FP), BF),
        ),
        in_specs=[any_spec()] * 4 + [vmem_spec()] * 2,
        out_specs=(any_spec(),) * 5,
        scratch_shapes=[
            pltpu.VMEM((2, D, FP), BF),
            pltpu.VMEM((FP, D), BF),
            pltpu.VMEM((1, D), BF),
            pltpu.VMEM((MICRO, LEN, D), BF),
            pltpu.VMEM((MICRO, LEN, D), BF),
            pltpu.VMEM((MICRO, LEN, D), BF),
            pltpu.VMEM((MICRO, LEN, FP), BF),
            pltpu.VMEM((MICRO, LEN, FP), BF),
            pltpu.VMEM((LEN, FP), BF),
            pltpu.VMEM((LEN, LEN), F32),
            pltpu.SemaphoreType.DMA((3,)),
            pltpu.SemaphoreType.DMA,
            pltpu.SemaphoreType.DMA((MICRO,)),
            pltpu.SemaphoreType.DMA((MICRO, 5)),
            pltpu.SemaphoreType.DMA((MICRO,)),
            pltpu.SemaphoreType.DMA((MICRO,)),
        ],
        compiler_params=pltpu.CompilerParams(
            collective_id=0, has_side_effects=True, vmem_limit_bytes=56 * MIB
        ),
        name="forward",
    )(tokens, flat, wide, tall, doc_col, doc_row)


def backward_kernel(
    cotangent, flat, wide, tall, doc_col, doc_row, inputs, first, second,
    d_inputs, grads, d_first, d_second, middle, d_gain,
    wide_v, tall_v, gain_v, g_v, z_v, dz_v, back_v, first_v, second_v, d_first_v, d_second_v, mid_v, dh_v, mask_v,
    weight_sem, gain_sem, in_sem, out_sem, send_sem, recv_sem,
):
    section = lax.axis_index("section")
    batch = lax.axis_index("batch")
    last = lax.axis_size("section") - 1
    barrier = pltpu.get_barrier_semaphore()

    @pl.when(section > 0)
    def _():
        pl.semaphore_signal(barrier, inc=1, device_id=(section - 1, batch), device_id_type=MESH)

    @pl.when(section < last)
    def _():
        pl.semaphore_signal(barrier, inc=1, device_id=(section + 1, batch), device_id_type=MESH)

    gain_copy = pltpu.make_async_copy(flat.at[:, pl.ds(0, D)], gain_v, gain_sem)
    gain_copy.start()
    wait_weights = load_weights(section, wide, tall, wide_v, tall_v, weight_sem)

    def rows_at(micro):
        return pl.ds(micro * LEN, LEN)

    def loads(micro):
        rows = rows_at(micro)
        return [
            pltpu.make_async_copy(inputs.at[rows, :], z_v.at[micro], in_sem.at[micro, 0]),
            pltpu.make_async_copy(first.at[rows, :], first_v.at[micro], in_sem.at[micro, 1]),
            pltpu.make_async_copy(second.at[rows, :], second_v.at[micro], in_sem.at[micro, 2]),
        ]

    def tangent_copy(micro):
        return pltpu.make_async_copy(cotangent.at[rows_at(micro), :], g_v.at[micro], in_sem.at[micro, 3])

    for micro in range(MICRO):
        for copy in loads(micro):
            copy.start()

        @pl.when(section == last)
        def _(micro=micro):
            tangent_copy(micro).start()

    pl.semaphore_wait(barrier, jnp.where((section > 0) & (section < last), 2, 1))
    gain_copy.wait()
    wait_weights()
    gain = 1.0 + gain_v[...].astype(F32) / 8.0
    d_gain[...] = jnp.zeros_like(d_gain)

    def hand_back(micro):
        return pltpu.make_async_remote_copy(
            src_ref=back_v.at[micro],
            dst_ref=g_v.at[micro],
            send_sem=send_sem.at[micro],
            recv_sem=recv_sem.at[micro],
            device_id=(section - 1, batch),
            device_id_type=MESH,
        )

    def feed(micro):
        def tile(t, carry):
            cols = at256(t)
            d_mid = dot_t(g_v[micro], tall_v[cols, :]) * SCALE
            gate = first_v[micro, :, cols].astype(F32)
            up = second_v[micro, :, cols].astype(F32)
            sig = 1.0 / (1.0 + jnp.exp(-gate))
            silu = gate * sig
            d_first_v[micro, :, cols] = (d_mid * up * (sig * (1.0 + gate * (1.0 - sig)))).astype(BF)
            d_second_v[micro, :, cols] = (d_mid * silu).astype(BF)
            mid_v[micro, :, cols] = (silu * up).astype(BF)
            return carry

        lax.fori_loop(0, FP // 256, tile, 0)

        def back(n, carry):
            rows = at256(n)
            total = dot_t(d_first_v[micro], wide_v[0, rows, :])
            total += dot_t(d_second_v[micro], wide_v[1, rows, :])
            dh_v[:, rows] = total * SCALE
            return carry

        lax.fori_loop(0, D // 256, back, 0)

    def attend(micro, kind):
        width = 2 * D if kind == WINDOW else 2 * HEADS * FEAT

        def mix(t, carry):
            rows = at256(t)
            mid_v[micro, :, rows] = (dot_t(g_v[micro], tall_v[rows, :]) * out_scale(kind)).astype(BF)
            return carry

        lax.fori_loop(0, D // 256, mix, 0)
        mask_v[...] = mask_of(kind, doc_col[micro], doc_row[micro])

        def block(t, d_low):
            queries = first_v[micro, :, query_block(kind, t)]
            keys = first_v[micro, :, key_block(kind, t)]
            values = second_v[micro, :, value_block(t)]
            d_mixed = mid_v[micro, :, value_block(t)]
            d_values = jnp.zeros((LEN, 128), F32)
            d_queries, d_keys = d_low
            for half in range(2):
                mask = mask_v[...]
                head = lane_of_head(kind, t, half)
                own_queries = only(head, queries)
                own_keys = only(head, keys)
                own_mixed = only(lane_of_value(half), d_mixed)
                scores = dot_t(own_queries, keys) * root_of(kind)
                weights, inverse = weigh(kind, scores, mask)
                d_weights = dot_t(own_mixed, values)
                d_values += dot_0(weights.astype(BF), own_mixed)
                d_scores = unweigh(kind, scores, mask, weights, inverse, d_weights).astype(BF)
                d_queries += dot(d_scores, own_keys)
                d_keys += dot_0(d_scores, own_queries)
            d_second_v[micro, :, value_block(t)] = d_values.astype(BF)
            return d_queries, d_keys

        zero = jnp.zeros((LEN, 128), F32)

        def store(t, d_low):
            d_queries, d_keys = d_low
            d_first_v[micro, :, query_block(kind, t)] = (d_queries * root_of(kind)).astype(BF)
            d_first_v[micro, :, key_block(kind, t)] = (d_keys * root_of(kind)).astype(BF)

        if kind == WINDOW:

            def whole(t, carry):
                store(t, block(t, (zero, zero)))
                return carry

            lax.fori_loop(0, 8, whole, 0)
        else:

            def group(q, carry):
                store(4 * q, lax.fori_loop(0, 4, lambda i, low: block(4 * q + i, low), (zero, zero)))
                return carry

            lax.fori_loop(0, 2, group, 0)

        def back(n, carry):
            rows = at256(n)
            total = dot_t(d_first_v[micro, :, pl.ds(0, width)], wide_v[0, rows, pl.ds(0, width)])
            total += dot_t(d_second_v[micro, :, pl.ds(0, D)], wide_v[1, rows, pl.ds(0, D)])
            dh_v[:, rows] = total * SCALE
            return carry

        lax.fori_loop(0, D // 256, back, 0)

    def unnorm(micro):
        z = z_v[micro].astype(F32)
        scaled = lax.rsqrt(jnp.mean(z * z, axis=1, keepdims=True) + EPSILON)
        unit = z * scaled
        d_normed = dh_v[...]
        d_gain[0:1, :] += jnp.sum(d_normed * unit, axis=0, keepdims=True) * 0.125
        d_unit = d_normed * gain
        d_z = scaled * (d_unit - unit * jnp.mean(d_unit * unit, axis=1, keepdims=True))
        d_z += g_v[micro].astype(F32)
        dz_v[micro] = d_z
        back_v[micro] = d_z.astype(BF)

    def outs(micro):
        rows = rows_at(micro)
        return [
            pltpu.make_async_copy(dz_v.at[micro], d_inputs.at[rows, :], out_sem.at[micro, 0]),
            pltpu.make_async_copy(g_v.at[micro], grads.at[rows, :], out_sem.at[micro, 1]),
            pltpu.make_async_copy(d_first_v.at[micro], d_first.at[rows, :], out_sem.at[micro, 2]),
            pltpu.make_async_copy(d_second_v.at[micro], d_second.at[rows, :], out_sem.at[micro, 3]),
            pltpu.make_async_copy(mid_v.at[micro], middle.at[rows, :], out_sem.at[micro, 4]),
        ]

    for micro in range(MICRO):
        for copy in loads(micro):
            copy.wait()

        @pl.when(section == last)
        def _(micro=micro):
            tangent_copy(micro).wait()

        @pl.when(section < last)
        def _(micro=micro):
            hand_back(micro).wait_recv()

        @pl.when(is_feed(section))
        def _(micro=micro):
            feed(micro)

        @pl.when(section == WINDOW)
        def _(micro=micro):
            attend(micro, WINDOW)

        @pl.when(section == LINEAR)
        def _(micro=micro):
            attend(micro, LINEAR)

        unnorm(micro)

        @pl.when(section > 0)
        def _(micro=micro):
            hand_back(micro).start()

        for copy in outs(micro):
            copy.start()

    for micro in range(MICRO):

        @pl.when(section > 0)
        def _(micro=micro):
            hand_back(micro).wait_send()

        for copy in outs(micro):
            copy.wait()


def backward(cotangent, flat, wide, tall, doc_col, doc_row, inputs, first, second):
    count = MICRO * LEN
    return pl.pallas_call(
        backward_kernel,
        out_shape=(
            jax.ShapeDtypeStruct((count, D), F32),
            jax.ShapeDtypeStruct((count, D), BF),
            jax.ShapeDtypeStruct((count, FP), BF),
            jax.ShapeDtypeStruct((count, FP), BF),
            jax.ShapeDtypeStruct((count, FP), BF),
            jax.ShapeDtypeStruct((8, D), F32),
        ),
        in_specs=[any_spec()] * 4 + [vmem_spec()] * 2 + [any_spec()] * 3,
        out_specs=(any_spec(),) * 5 + (vmem_spec(),),
        scratch_shapes=[
            pltpu.VMEM((2, D, FP), BF),
            pltpu.VMEM((FP, D), BF),
            pltpu.VMEM((1, D), BF),
            pltpu.VMEM((MICRO, LEN, D), BF),
            pltpu.VMEM((MICRO, LEN, D), BF),
            pltpu.VMEM((MICRO, LEN, D), F32),
            pltpu.VMEM((MICRO, LEN, D), BF),
            pltpu.VMEM((MICRO, LEN, FP), BF),
            pltpu.VMEM((MICRO, LEN, FP), BF),
            pltpu.VMEM((MICRO, LEN, FP), BF),
            pltpu.VMEM((MICRO, LEN, FP), BF),
            pltpu.VMEM((MICRO, LEN, FP), BF),
            pltpu.VMEM((LEN, D), F32),
            pltpu.VMEM((LEN, LEN), F32),
            pltpu.SemaphoreType.DMA((3,)),
            pltpu.SemaphoreType.DMA,
            pltpu.SemaphoreType.DMA((MICRO, 4)),
            pltpu.SemaphoreType.DMA((MICRO, 5)),
            pltpu.SemaphoreType.DMA((MICRO,)),
            pltpu.SemaphoreType.DMA((MICRO,)),
        ],
        compiler_params=pltpu.CompilerParams(
            collective_id=1, has_side_effects=True, vmem_limit_bytes=56 * MIB
        ),
        name="backward",
    )(cotangent, flat, wide, tall, doc_col, doc_row, inputs, first, second)


HEAD_ROWS = 16
PAIR_ROWS = 128 * 43


def flip(source, rows, width, target):
    def piece(t, carry):
        cols = pl.ds(pl.multiple_of(t * 128, 128), 128)
        target[cols, :] = source[:, cols].astype(F32).T.astype(target.dtype)
        return carry

    lax.fori_loop(0, width // 128, piece, 0)


def products_kernel(
    normed, d_first, d_second, middle, second, grads, d_gain, out,
    h_v, d_v, shift_v, m_v, g_v, turned, even, odd, m_turned, stage, packed, in_sem, out_sem,
):
    section = lax.axis_index("section")
    count = MICRO * LEN

    def fetch(source, target, index):
        return pltpu.make_async_copy(source, target, in_sem.at[index])

    shared = [fetch(normed, h_v, 0), fetch(grads, g_v, 1), fetch(d_first, d_v.at[0], 2), fetch(d_second, d_v.at[1], 3)]
    for copy in shared:
        copy.start()
    own_middle = fetch(middle, m_v, 4)
    own_mixed = fetch(second.at[:, pl.ds(D, D)], m_v.at[:, pl.ds(0, D)], 4)

    @pl.when(is_feed(section))
    def _():
        own_middle.start()

    @pl.when(jnp.logical_not(is_feed(section)))
    def _():
        own_mixed.start()

    def put(slot, first_row, rows):
        return pltpu.make_async_copy(
            packed.at[slot, pl.ds(0, rows), :], out.at[pl.ds(first_row, rows), :], out_sem.at[slot]
        )

    stage[pl.ds(0, 8), :] = jnp.zeros((8, 128), F32)
    stage[pl.ds(8, 8), :] = d_gain[0:1, :].reshape(8, 128)
    packed[0, pl.ds(0, 16), :] = stage[pl.ds(0, 16), :].astype(BF)
    head = put(0, 0, HEAD_ROWS)
    head.start()
    head.wait()

    def emit(steps, rows, first_row, work):
        def place(i):
            return pl.multiple_of(HEAD_ROWS + first_row + i * rows, 16)

        def step(i, carry):
            slot = lax.rem(i, 2)
            work(i)

            @pl.when(i >= 2)
            def _():
                put(slot, place(i - 2), rows).wait()

            def cut(j, inner):
                piece = pl.ds(pl.multiple_of(j * 32, 32), 32)
                packed[slot, piece, :] = stage[piece, :].astype(BF)
                return inner

            lax.fori_loop(0, rows // 32, cut, 0, unroll=4)
            put(slot, place(i), rows).start()
            return carry

        lax.fori_loop(0, steps, step, 0)
        for i in range(max(steps - 2, 0), steps):
            put(i % 2, place(i), rows).wait()

    def zeros(first_row, rows):
        packed[0, pl.ds(0, 512), :] = jnp.zeros((512, 128), BF)

        def place(i):
            return pl.multiple_of(HEAD_ROWS + first_row + i * 512, 16)

        def start(i, carry):
            put(0, place(i), 512).start()
            put(0, place(i), 512).wait()
            return carry

        lax.fori_loop(0, rows // 512, start, 0)

    for copy in shared:
        copy.wait()

    def tall_product(turned_ref, rows, step_rows, scale):
        def work(i):
            def tile(j, carry):
                left = turned_ref[pl.ds(pl.multiple_of(i * step_rows, 16), step_rows), :]
                piece = dot(left, g_v[:, at256(j)]) * scale
                stage[pl.ds(2 * j, step_rows, stride=8), :] = piece[:, :128]
                stage[pl.ds(2 * j + 1, step_rows, stride=8), :] = piece[:, 128:]
                return carry

            lax.fori_loop(0, 4, tile, 0)

        return work

    def wide_product(which, first_col, width, step_rows):
        stride = width // 128

        def work(i):
            def tile(j, carry):
                left = turned[pl.ds(pl.multiple_of(i * step_rows, 16), step_rows), :]
                cols = pl.ds(pl.multiple_of(first_col + j * 256, 256), 256)
                piece = dot(left, d_v[which, :, cols]) * SCALE
                stage[pl.ds(2 * j, step_rows, stride=stride), :] = piece[:, :128]
                stage[pl.ds(2 * j + 1, step_rows, stride=stride), :] = piece[:, 128:]
                return carry

            lax.fori_loop(0, width // 256, tile, 0)

        return work

    @pl.when(is_feed(section))
    def _():
        own_middle.wait()
        flip(m_v, count, FP, m_turned)

        def halves(t, carry):
            cols = pl.ds(pl.multiple_of(t * 128, 128), 128)
            stage[pl.ds(0, 512), :] = h_v[:, cols].astype(F32)
            for part in range(4):
                turned_piece = stage[pl.ds(128 * part, 128), :].T
                shift_v[0, pl.ds(0, 128), pl.ds(128 * part, 128)] = turned_piece.astype(BF)
                stage[pl.ds(512 + 128 * part, 128), :] = turned_piece
                rows = pl.ds(pl.multiple_of(t * 64, 64), 64)
                even[rows, pl.ds(128 * part, 128)] = stage[pl.ds(512 + 128 * part, 64, stride=2), :].astype(BF)
                odd[rows, pl.ds(128 * part, 128)] = stage[pl.ds(513 + 128 * part, 64, stride=2), :].astype(BF)
            return carry

        lax.fori_loop(0, 8, halves, 0)

        low_half = lax.broadcasted_iota(jnp.int32, (1, 128), 1) < 64

        for which in range(2):

            def shift(t, before, which=which):
                cols = pl.ds(pl.multiple_of(t * 128, 128), 128)
                here = pltpu.roll(d_v[which, :, cols].astype(F32), 64, 1)
                shift_v[which, :, cols] = jnp.where(low_half, before, here).astype(BF)
                return here

            lax.fori_loop(0, FP // 128, shift, jnp.zeros((count, 128), F32))

        def pairs(i):
            which = i // 4
            rows = pl.ds(pl.multiple_of(lax.rem(i, 4) * 128, 128), 128)

            def even_tile(j, carry):
                piece = dot(even[rows, :], d_v[which, :, at256(j)]) * SCALE
                stage[pl.ds(2 * j, 128, stride=43), :] = piece[:, :128]
                stage[pl.ds(2 * j + 1, 128, stride=43), :] = piece[:, 128:]
                return carry

            lax.fori_loop(0, FP // 256, even_tile, 0)
            piece = dot(odd[rows, :], shift_v[which, :, pl.ds(0, 256)]) * SCALE
            stage[pl.ds(21, 128, stride=43), :] += piece[:, :128]
            stage[pl.ds(22, 128, stride=43), :] = piece[:, 128:]

            def odd_tile(j, carry):
                piece = dot(odd[rows, :], shift_v[which, :, at256(j)]) * SCALE
                stage[pl.ds(21 + 2 * j, 128, stride=43), :] = piece[:, :128]
                stage[pl.ds(22 + 2 * j, 128, stride=43), :] = piece[:, 128:]
                return carry

            lax.fori_loop(1, FP // 256, odd_tile, 0)

        emit(8, PAIR_ROWS, 0, pairs)
        emit(4, PAIR_ROWS, 8 * PAIR_ROWS, tall_product(m_turned, FF, 688, SCALE))

    def attention(kind):
        own_mixed.wait()
        flip(h_v, count, D, turned)
        flip(m_v, count, D, m_turned)
        low = D if kind == WINDOW else HEADS * FEAT
        low_rows = 8 * low
        step_rows = 1024 * 128 // low
        for part in range(2):
            emit(low_rows // 1024, 1024, part * low_rows, wide_product(0, part * low, low, step_rows))
        emit(8, 1024, 2 * low_rows, wide_product(1, 0, D, 128))
        emit(8, 1024, 2 * low_rows + 8192, tall_product(m_turned, D, 128, out_scale(kind)))
        done = 2 * low_rows + 16384
        zeros(done, 66048 - done)

    @pl.when(section == WINDOW)
    def _():
        attention(WINDOW)

    @pl.when(section == LINEAR)
    def _():
        attention(LINEAR)


def products(normed, d_first, d_second, middle, second, grads, d_gain, total_rows):
    count = MICRO * LEN
    return pl.pallas_call(
        products_kernel,
        out_shape=jax.ShapeDtypeStruct((total_rows, 128), BF),
        in_specs=[any_spec()] * 6 + [vmem_spec()],
        out_specs=any_spec(),
        scratch_shapes=[
            pltpu.VMEM((count, D), BF),
            pltpu.VMEM((2, count, FP), BF),
            pltpu.VMEM((2, count, FP), BF),
            pltpu.VMEM((count, FP), BF),
            pltpu.VMEM((count, D), BF),
            pltpu.VMEM((D, count), BF),
            pltpu.VMEM((512, count), BF),
            pltpu.VMEM((512, count), BF),
            pltpu.VMEM((FP, count), BF),
            pltpu.VMEM((PAIR_ROWS, 128), F32),
            pltpu.VMEM((2, PAIR_ROWS, 128), BF),
            pltpu.SemaphoreType.DMA((5,)),
            pltpu.SemaphoreType.DMA((2,)),
        ],
        compiler_params=pltpu.CompilerParams(vmem_limit_bytes=56 * MIB),
        name="products",
    )(normed, d_first, d_second, middle, second, grads, d_gain)


def document_ids(lengths):
    ends = jnp.cumsum(lengths, axis=1)
    places = jnp.arange(LEN, dtype=jnp.int32)
    return jnp.sum((places[None, :, None] >= ends[:, None, :]).astype(jnp.int32), axis=2)


def shards(tokens, cotangent, params, lengths):
    docs = document_ids(lengths[0])
    doc_col, doc_row = docs[:, :, None], docs[:, None, :]
    wide, tall = prepare(params)
    acts, inputs, normed, first, second = forward(tokens, params, wide, tall, doc_col, doc_row)
    d_inputs, grads, d_first, d_second, middle, d_gain = backward(
        cotangent, params, wide, tall, doc_col, doc_row, inputs, first, second
    )
    total_rows = params.shape[1] // 128 + 8
    parts = products(normed, d_first, d_second, middle, second, grads, d_gain, total_rows)
    mine = lax.psum_scatter(parts[8:].reshape(-1), "batch", scatter_dimension=0, tiled=True)
    return acts[None], d_inputs[None], mine.astype(F32)[None]


def solution(mesh):
    return jax.shard_map(
        shards,
        mesh=mesh,
        in_specs=(P("batch", None), P("batch", None), P("section", None), P("batch", None, None)),
        out_specs=(P("section", "batch", None), P("section", "batch", None), P("section", "batch")),
        check_vma=False,
    )
```

time: 2330 us -> 739 us (0.32)
  waiting for transfers between devices: 1270 us -> 334 us
  other arithmetic: 429 us -> 2.65 us
  Pallas kernels: 0 us -> 340 us
  loops' own time: 257 us -> 0 us
  local copies, waits for them, and re-layouts: 182 us -> 44.2 us
  starting transfers between devices: 107 us -> 0.04 us
  matrix products: 52.1 us -> 0 us
    ppermute x8 -> x0, waiting for transfers between devices: 644 us -> none  [shifted(): return lax.ppermute(block, axis, route)]
    unnamed x1 -> x0, other arithmetic: 358 us -> none
    pallas_call x0 -> x4, Pallas kernels: none -> 340 us  [the longest x1 152 us: backward(): pl.pallas_call(backward_kernel, out_shape=(jax.ShapeDtypeStruct((count, D...]
    unnamed x2, waiting for transfers between devices: 622 us -> 334 us
    another operation x10 -> x0, loops' own time: 257 us -> none  [the longest x5 163 us: shards(): lax.switch(branch_pick, backward_fns, flat, stashed[place], doc_table[pla...]
    ppermute x8 -> x0, starting transfers between devices: 106 us -> none  [shifted(): return lax.ppermute(block, axis, route)]
    slice x24 -> x0, local copies, waits for them, and re-layouts: 69.1 us -> none  [unpack(): flat[offset:offset + row_count * col_count].reshape(row_count, col_count)]
    cond x32 -> x0, local copies, waits for them, and re-layouts: 56.3 us -> none
  transfers between devices with their start and end apart: 9 -> 1, of which waited for: 9 -> 1; matrix products, arithmetic and copies ran while one was open for 1% -> 0% of each run, Pallas kernels for 0% -> 0%
where the time goes in v1:
time: 739 us; the launch traced here: 736 us
  Pallas kernels  340 us (46%)
  waiting for transfers between devices  334 us (45%)
  local copies, waits for them, and re-layouts  44.2 us (6%)
  between operations  14.8 us (2%)
    unnamed x2, waiting for transfers between devices  334 us
    pallas_call x1, Pallas kernels, backward(): pl.pallas_call(backward_kernel, out_shape=(jax.ShapeDtypeStruct((count, D...  152 us
    pallas_call x1, Pallas kernels, products(): pl.pallas_call(products_kernel, out_shape=jax.ShapeDtypeStruct((total_row...  82.4 us
    pallas_call x1, Pallas kernels, forward(): pl.pallas_call(forward_kernel, out_shape=(jax.ShapeDtypeStruct((count, D)...  82.1 us
    pallas_call x1, Pallas kernels, prepare(): pl.pallas_call(prepare_kernel, out_shape=(jax.ShapeDtypeStruct((2, D, FP)...  23.6 us
    broadcast_in_dim x1, local copies, waits for them, and re-layouts, shards(): return (acts[None], d_inputs[None], mine.astype(F32)[None])  20.6 us
  transfers between devices with their start and end apart: 1, of which 1 were waited for; matrix products, arithmetic and copies ran while one was open for 0% of the time, Pallas kernels for 0%

profile of v1, /device:TPU:8, one launch (start us, length us, event | category | flops | bytes accessed | tf_op | source)
XLA Modules:
  0.0 735.5 jit_solution(9243082001400025089)
XLA Ops:
  7.2 0.0 copy-start.4
  7.2 0.0 all-reduce.3.cloned.1.call-start
  7.2 23.6 %prepare.1 = (bf16[2,1024,2816]{2,1,0:T(8,128)(2,1)S(1)}, bf16[2816,1024]{1,0:T(8,128)(2,1)S(1)}) custom-call(bf16[1,8455168]{1,0:T(2,128)(2,1)} %flat.5), custom_call_target="tpu_custom_call" | custom-call | tf_op jit(solution)/shard_map/prepare/pallas_call | solution.py:180
  30.9 0.0 copy-start
  30.9 4.3 copy-done
  35.2 2.4 copy-done.1
  37.7 0.0 copy-done.4
  37.7 0.2 reduce_window_sum.14
  37.8 0.1 convert_reduce_fusion
  37.9 0.6 broadcast_in_dim.21.doc_row
  38.5 0.9 copy.11.doc_col
  39.4 82.1 %forward.1 = (bf16[512,1024]{1,0:T(8,128)(2,1)}, bf16[512,1024]{1,0:T(8,128)(2,1)}, bf16[512,1024]{1,0:T(8,128)(2,1)}, bf16[512,2816]{1,0:T(8,128)(2,1)}, bf16[512,2816]{1,0:T(8,128)(2,1)}) custom-call(bf16[512,1024]{1,0:T(8,128)(2,1)} %tokens.1, bf16[1,8455168]{1,0:T(2,128)(2,1)} %flat.5, bf16[2,1024,2816]{2,1,0:T(8,128)(2,1)} %copy-done, ...), custom_call_target="tpu_custom_call" | custom-call | tf_op jit(solution)/shard_map/forward/pallas_call | solution.py:450
  121.5 151.7 %backward.1 = (f32[512,1024]{1,0:T(8,128)}, bf16[512,1024]{1,0:T(8,128)(2,1)}, bf16[512,2816]{1,0:T(8,128)(2,1)}, bf16[512,2816]{1,0:T(8,128)(2,1)}, bf16[512,2816]{1,0:T(8,128)(2,1)}, /*index=5*/f32[8,1024]{1,0:T(8,128)}) custom-call(bf16[512,1024]{1,0:T(8,128)(2,1)} %cotangent.1, bf16[1,8455168]{1,0:T(2,128)(2,1)} %flat.5, bf16[2,1024,2816]{2,1,0:T(8,128)(2,1)} %copy-done, ...), custom_call_target="tpu_custom_call" | custom-call | tf_op jit(solution)/shard_map/backward/pallas_call | solution.py:703
  273.3 82.4 %products.1 = bf16[66064,128]{1,0:T(8,128)(2,1)} custom-call(bf16[512,1024]{1,0:T(8,128)(2,1)} %get-tuple-element.23.normed, bf16[512,2816]{1,0:T(8,128)(2,1)} %get-tuple-element.24.d_first, bf16[512,2816]{1,0:T(8,128)(2,1)} %get-tuple-element.25.d_second, bf16[512,2816]{1,0:T(8,128)(2,1)} %get-tuple-element.26.middle, ...), custom_call_target="tpu_custom_call" | custom-call | tf_op jit(solution)/shard_map/products/pallas_call | solution.py:945
  355.7 11.9 %slice_bitcast_fusion = bf16[8455168]{0:T(1024)(128)(2,1)} fusion(bf16[66064,128]{1,0:T(8,128)(2,1)} %products.1), kind=kLoop, calls=%fused_computation | loop fusion | bytes 33820672 | tf_op jit(solution)/shard_map/reshape | solution.py:986
  367.6 0.0 all-reduce.3.cloned.1.call-update
  367.6 0.6 copy-done.5
  368.2 0.6 dynamic-slice
  369.5 333.9 %all-reduce.3.cloned.1.call-done = bf16[8455168]{0:T(1024)(128)(2,1)} async-done(((bf16[8455168]{0:T(1024)(128)(2,1)}), bf16[8455168]{0:T(1024)(128)(2,1)}) %all-reduce.3.cloned.1.call-update) | async-done | bytes 16910352
  703.4 2.4 dynamic-slice_convert_fusion
  705.8 0.0 copy-start.3
  705.8 20.6 %reshape.14 = f32[1,1056896]{1,0:T(1,128)} reshape(f32[1056896]{0:T(1024)S(1)} %dynamic-slice_convert_fusion) | data formatting | bytes 8455168 | tf_op jit(solution)/shard_map/broadcast_in_dim | solution.py:987
  726.4 1.0 copy.16
  727.4 1.3 copy.17
  (5 shorter events, 0.0 us)
Async XLA Ops:
  7.2 30.5 %copy-start.4 = (s32[1,2,4]{2,1,0:T(2,128)S(1)}, s32[1,2,4]{2,1,0:T(2,128)}, u32[]{:S(2)}) copy-start(s32[1,2,4]{2,1,0:T(2,128)} %param.7) | copy-start | bytes 100
  7.2 696.2 %all-reduce.3.cloned.1.call-start = ((), (), s32[]{:S(2)}) async-start(), calls=%async_computation | async-start | bytes 33820672
  30.9 4.3 copy-start
  35.2 2.4 copy-start.1
  367.6 0.7 copy-start.5
  705.8 20.6 %copy-start.3 = (bf16[512,1024]{1,0:T(8,128)(2,1)S(1)}, bf16[512,1024]{1,0:T(8,128)(2,1)}, u32[]{:S(2)}) copy-start(bf16[512,1024]{1,0:T(8,128)(2,1)} %get-tuple-element.18) | copy-start | bytes 3145732
  705.8 21.6 %copy-start.2 = (f32[512,1024]{1,0:T(8,128)S(1)}, f32[512,1024]{1,0:T(8,128)}, u32[]{:S(2)}) copy-start(f32[512,1024]{1,0:T(8,128)} %get-tuple-element.22) | copy-start | bytes 6291460
Sparse Core Ops, SparseCore 0:
  367.7 335.6 all-reduce.2

commit v2 on v1

--- a/solution.py
+++ b/solution.py
@@ -743,228 +743,494 @@
 
 HEAD_ROWS = 16
 PAIR_ROWS = 128 * 43
-
-
-def flip(source, rows, width, target):
+CHUNKS = 11
+
+
+def flip(source, first, width, target):
     def piece(t, carry):
         cols = pl.ds(pl.multiple_of(t * 128, 128), 128)
-        target[cols, :] = source[:, cols].astype(F32).T.astype(target.dtype)
+        rows = pl.ds(pl.multiple_of(first + t * 128, 128), 128)
+        target[rows, :] = source[:, cols].astype(F32).T.astype(target.dtype)
         return carry
 
     lax.fori_loop(0, width // 128, piece, 0)
 
 
-def products_kernel(
-    normed, d_first, d_second, middle, second, grads, d_gain, out,
-    h_v, d_v, shift_v, m_v, g_v, turned, even, odd, m_turned, stage, packed, in_sem, out_sem,
-):
-    section = lax.axis_index("section")
-    count = MICRO * LEN
-
-    def fetch(source, target, index):
-        return pltpu.make_async_copy(source, target, in_sem.at[index])
-
-    shared = [fetch(normed, h_v, 0), fetch(grads, g_v, 1), fetch(d_first, d_v.at[0], 2), fetch(d_second, d_v.at[1], 3)]
-    for copy in shared:
-        copy.start()
-    own_middle = fetch(middle, m_v, 4)
-    own_mixed = fetch(second.at[:, pl.ds(D, D)], m_v.at[:, pl.ds(0, D)], 4)
-
-    @pl.when(is_feed(section))
-    def _():
-        own_middle.start()
-
-    @pl.when(jnp.logical_not(is_feed(section)))
-    def _():
-        own_mixed.start()
-
-    def put(slot, first_row, rows):
-        return pltpu.make_async_copy(
-            packed.at[slot, pl.ds(0, rows), :], out.at[pl.ds(first_row, rows), :], out_sem.at[slot]
-        )
-
-    stage[pl.ds(0, 8), :] = jnp.zeros((8, 128), F32)
-    stage[pl.ds(8, 8), :] = d_gain[0:1, :].reshape(8, 128)
-    packed[0, pl.ds(0, 16), :] = stage[pl.ds(0, 16), :].astype(BF)
-    head = put(0, 0, HEAD_ROWS)
-    head.start()
-    head.wait()
-
-    def emit(steps, rows, first_row, work):
-        def place(i):
-            return pl.multiple_of(HEAD_ROWS + first_row + i * rows, 16)
-
-        def step(i, carry):
-            slot = lax.rem(i, 2)
-            work(i)
-
-            @pl.when(i >= 2)
-            def _():
-                put(slot, place(i - 2), rows).wait()
-
-            def cut(j, inner):
-                piece = pl.ds(pl.multiple_of(j * 32, 32), 32)
-                packed[slot, piece, :] = stage[piece, :].astype(BF)
-                return inner
-
-            lax.fori_loop(0, rows // 32, cut, 0, unroll=4)
-            put(slot, place(i), rows).start()
-            return carry
-
-        lax.fori_loop(0, steps, step, 0)
-        for i in range(max(steps - 2, 0), steps):
-            put(i % 2, place(i), rows).wait()
-
-    def zeros(first_row, rows):
-        packed[0, pl.ds(0, 512), :] = jnp.zeros((512, 128), BF)
-
-        def place(i):
-            return pl.multiple_of(HEAD_ROWS + first_row + i * 512, 16)
-
-        def start(i, carry):
-            put(0, place(i), 512).start()
-            put(0, place(i), 512).wait()
-            return carry
-
-        lax.fori_loop(0, rows // 512, start, 0)
-
-    for copy in shared:
-        copy.wait()
-
-    def tall_product(turned_ref, rows, step_rows, scale):
-        def work(i):
-            def tile(j, carry):
-                left = turned_ref[pl.ds(pl.multiple_of(i * step_rows, 16), step_rows), :]
-                piece = dot(left, g_v[:, at256(j)]) * scale
-                stage[pl.ds(2 * j, step_rows, stride=8), :] = piece[:, :128]
-                stage[pl.ds(2 * j + 1, step_rows, stride=8), :] = piece[:, 128:]
-                return carry
-
-            lax.fori_loop(0, 4, tile, 0)
-
-        return work
-
-    def wide_product(which, first_col, width, step_rows):
-        stride = width // 128
-
-        def work(i):
-            def tile(j, carry):
-                left = turned[pl.ds(pl.multiple_of(i * step_rows, 16), step_rows), :]
-                cols = pl.ds(pl.multiple_of(first_col + j * 256, 256), 256)
-                piece = dot(left, d_v[which, :, cols]) * SCALE
-                stage[pl.ds(2 * j, step_rows, stride=stride), :] = piece[:, :128]
-                stage[pl.ds(2 * j + 1, step_rows, stride=stride), :] = piece[:, 128:]
-                return carry
-
-            lax.fori_loop(0, width // 256, tile, 0)
-
-        return work
-
-    @pl.when(is_feed(section))
-    def _():
-        own_middle.wait()
-        flip(m_v, count, FP, m_turned)
+class Products:
+    def __init__(self, sources, scratch):
+        self.normed, self.d_first, self.d_second, self.middle, self.second, self.grads, self.d_gain = sources
+        self.h_v, self.d_v, self.m_v, self.g_v, self.turned, self.m_turned, self.stage, self.in_sem = scratch
+
+    def fetch(self, source, target, index):
+        return pltpu.make_async_copy(source, target, self.in_sem.at[index])
+
+    def shared(self):
+        return [
+            self.fetch(self.normed, self.h_v, 0),
+            self.fetch(self.grads, self.g_v, 1),
+            self.fetch(self.d_first, self.d_v.at[0], 2),
+            self.fetch(self.d_second, self.d_v.at[1], 3),
+        ]
+
+    def middle_half(self, part):
+        half = FP // 2
+        return self.fetch(self.middle.at[:, pl.ds(part * half, half)], self.m_v, 4)
+
+    def mixed(self):
+        return self.fetch(self.second.at[:, pl.ds(D, D)], self.m_v.at[:, pl.ds(0, D)], 4)
+
+    def head(self, out):
+        stage = self.stage
+        stage[pl.ds(0, 8), :] = jnp.zeros((8, 128), F32)
+        stage[pl.ds(8, 8), :] = self.d_gain[0:1, :].reshape(8, 128)
+        out[pl.ds(0, 16), :] = stage[pl.ds(0, 16), :].astype(BF)
+
+    def cut(self, out, first_row, rows, piece):
+        def step(j, carry):
+            source = pl.ds(pl.multiple_of(j * piece, 16), piece)
+            target = pl.ds(pl.multiple_of(first_row + j * piece, 16), piece)
+            out[target, :] = self.stage[source, :].astype(BF)
+            return carry
+
+        lax.fori_loop(0, rows // piece, step, 0)
+
+    def start_feed(self):
+        self.middle_half(0).start()
+        for copy in self.shared():
+            copy.wait()
+        stage = self.stage
 
         def halves(t, carry):
             cols = pl.ds(pl.multiple_of(t * 128, 128), 128)
-            stage[pl.ds(0, 512), :] = h_v[:, cols].astype(F32)
+            stage[pl.ds(0, 512), :] = self.h_v[:, cols].astype(F32)
             for part in range(4):
-                turned_piece = stage[pl.ds(128 * part, 128), :].T
-                shift_v[0, pl.ds(0, 128), pl.ds(128 * part, 128)] = turned_piece.astype(BF)
-                stage[pl.ds(512 + 128 * part, 128), :] = turned_piece
-                rows = pl.ds(pl.multiple_of(t * 64, 64), 64)
-                even[rows, pl.ds(128 * part, 128)] = stage[pl.ds(512 + 128 * part, 64, stride=2), :].astype(BF)
-                odd[rows, pl.ds(128 * part, 128)] = stage[pl.ds(513 + 128 * part, 64, stride=2), :].astype(BF)
+                stage[pl.ds(512 + 128 * part, 128), :] = stage[pl.ds(128 * part, 128), :].T
+            for part in range(4):
+                for odd in range(2):
+                    rows = pl.ds(pl.multiple_of(512 * odd + t * 64, 64), 64)
+                    piece = stage[pl.ds(512 + 128 * part + odd, 64, stride=2), :]
+                    self.turned[rows, pl.ds(128 * part, 128)] = piece.astype(BF)
             return carry
 
         lax.fori_loop(0, 8, halves, 0)
-
-        low_half = lax.broadcasted_iota(jnp.int32, (1, 128), 1) < 64
-
-        for which in range(2):
-
-            def shift(t, before, which=which):
-                cols = pl.ds(pl.multiple_of(t * 128, 128), 128)
-                here = pltpu.roll(d_v[which, :, cols].astype(F32), 64, 1)
-                shift_v[which, :, cols] = jnp.where(low_half, before, here).astype(BF)
-                return here
-
-            lax.fori_loop(0, FP // 128, shift, jnp.zeros((count, 128), F32))
-
-        def pairs(i):
-            which = i // 4
-            rows = pl.ds(pl.multiple_of(lax.rem(i, 4) * 128, 128), 128)
-
-            def even_tile(j, carry):
-                piece = dot(even[rows, :], d_v[which, :, at256(j)]) * SCALE
-                stage[pl.ds(2 * j, 128, stride=43), :] = piece[:, :128]
-                stage[pl.ds(2 * j + 1, 128, stride=43), :] = piece[:, 128:]
-                return carry
-
-            lax.fori_loop(0, FP // 256, even_tile, 0)
-            piece = dot(odd[rows, :], shift_v[which, :, pl.ds(0, 256)]) * SCALE
-            stage[pl.ds(21, 128, stride=43), :] += piece[:, :128]
-            stage[pl.ds(22, 128, stride=43), :] = piece[:, 128:]
-
-            def odd_tile(j, carry):
-                piece = dot(odd[rows, :], shift_v[which, :, at256(j)]) * SCALE
-                stage[pl.ds(21 + 2 * j, 128, stride=43), :] = piece[:, :128]
-                stage[pl.ds(22 + 2 * j, 128, stride=43), :] = piece[:, 128:]
-                return carry
-
-            lax.fori_loop(1, FP // 256, odd_tile, 0)
-
-        emit(8, PAIR_ROWS, 0, pairs)
-        emit(4, PAIR_ROWS, 8 * PAIR_ROWS, tall_product(m_turned, FF, 688, SCALE))
-
-    def attention(kind):
-        own_mixed.wait()
-        flip(h_v, count, D, turned)
-        flip(m_v, count, D, m_turned)
-        low = D if kind == WINDOW else HEADS * FEAT
-        low_rows = 8 * low
-        step_rows = 1024 * 128 // low
+        half = FP // 2
         for part in range(2):
-            emit(low_rows // 1024, 1024, part * low_rows, wide_product(0, part * low, low, step_rows))
-        emit(8, 1024, 2 * low_rows, wide_product(1, 0, D, 128))
-        emit(8, 1024, 2 * low_rows + 8192, tall_product(m_turned, D, 128, out_scale(kind)))
-        done = 2 * low_rows + 16384
-        zeros(done, 66048 - done)
+            self.middle_half(part).wait()
+            flip(self.m_v, part * half, half, self.m_turned)
+            if part == 0:
+                self.middle_half(1).start()
+
+    def pairs(self, out, which, first_pair, count, first_row):
+        stage = self.stage
+        half = FP // 2
+        low_half = lax.broadcasted_iota(jnp.int32, (count, 128), 1) < 64
+        even = self.turned[pl.ds(pl.multiple_of(first_pair, 16), count), :]
+        odd = self.turned[pl.ds(pl.multiple_of(512 + first_pair, 16), count), :]
+        for part in range(2):
+            piece = dot(even, self.d_v[which, :, pl.ds(part * half, half)]) * SCALE
+            for c in range(11):
+                stage[pl.ds(11 * part + c, count, stride=43), :] = piece[:, 128 * c : 128 * c + 128]
+        before = stage[pl.ds(21, count, stride=43), :]
+        for part in range(2):
+            piece = dot(odd, self.d_v[which, :, pl.ds(part * half, half)]) * SCALE
+            for c in range(11):
+                here = pltpu.roll(piece[:, 128 * c : 128 * c + 128], 64, 1)
+                stage[pl.ds(21 + 11 * part + c, count, stride=43), :] = jnp.where(low_half, before, here)
+                before = here
+        self.cut(out, first_row, 43 * count, 688)
+
+    def tall(self, out, left, right, stride, rows, first_row, scale, piece):
+        product = dot(left, right) * scale
+        for c in range(stride):
+            self.stage[pl.ds(c, rows, stride=stride), :] = product[:, 128 * c : 128 * c + 128]
+        self.cut(out, first_row, rows * stride, piece)
+
+    def down(self, out, first_channel, rows, first_row, piece):
+        left = self.m_turned[pl.ds(pl.multiple_of(first_channel, 16), rows), :]
+        self.tall(out, left, self.g_v[...], 8, rows, first_row, SCALE, piece)
+
+    def feed_tile(self, out, k):
+        first_row = pl.multiple_of(HEAD_ROWS + k * PAIR_ROWS, 16)
+
+        @pl.when(k < 8)
+        def _():
+            self.pairs(out, k // 4, lax.rem(k, 4) * 128, 128, first_row)
+
+        @pl.when(k >= 8)
+        def _():
+            self.down(out, (k - 8) * 688, 688, first_row, 688)
+
+    def start_attention(self):
+        self.mixed().start()
+        for copy in self.shared():
+            copy.wait()
+        flip(self.h_v, 0, D, self.turned)
+        self.mixed().wait()
+        flip(self.m_v, 0, D, self.m_turned)
+
+    def square(self, out, left, right, first_row, scale):
+        def step(i, carry):
+            rows = pl.ds(pl.multiple_of(i * 512, 512), 512)
+            self.tall(out, left[rows, :], right(), 8, 512, pl.multiple_of(first_row + i * 4096, 16), scale, 512)
+            return carry
+
+        lax.fori_loop(0, 2, step, 0)
+
+    def window(self, out, part):
+        first_row = HEAD_ROWS + part * 8192
+        if part < 3:
+            cols = pl.ds(D if part == 1 else 0, D)
+            self.square(out, self.turned, lambda: self.d_v[part // 2, :, cols], first_row, SCALE)
+        else:
+            self.square(out, self.m_turned, lambda: self.g_v[...], first_row, out_scale(WINDOW))
+
+    def linear(self, out):
+        width = HEADS * FEAT
+        for part in range(2):
+            right = self.d_v[0, :, pl.ds(part * width, width)]
+            self.tall(out, self.turned[...], right, 2, D, HEAD_ROWS + part * 2048, SCALE, 512)
+        self.square(out, self.turned, lambda: self.d_v[1, :, pl.ds(0, D)], HEAD_ROWS + 4096, SCALE)
+        self.square(out, self.m_turned, lambda: self.g_v[...], HEAD_ROWS + 12288, out_scale(LINEAR))
+
+
+def product_scratch():
+    count = MICRO * LEN
+    return [
+        pltpu.VMEM((count, D), BF),
+        pltpu.VMEM((2, count, FP), BF),
+        pltpu.VMEM((count, FP // 2), BF),
+        pltpu.VMEM((count, D), BF),
+        pltpu.VMEM((D, count), BF),
+        pltpu.VMEM((FP, count), BF),
+        pltpu.VMEM((PAIR_ROWS, 128), F32),
+        pltpu.SemaphoreType.DMA((5,)),
+    ]
+
+
+def clear(out, first_row, rows):
+    def step(i, carry):
+        out[pl.ds(pl.multiple_of(first_row + i * 128, 16), 128), :] = jnp.zeros((128, 128), BF)
+        return carry
+
+    lax.fori_loop(0, rows // 128, step, 0)
+    if rows % 128:
+        out[pl.ds(first_row + rows // 128 * 128, rows % 128), :] = jnp.zeros((rows % 128, 128), BF)
+
+
+def products_kernel(*refs):
+    section = lax.axis_index("section")
+    work = Products(refs[:7], refs[9:])
+    out, out_v = refs[7:9]
+    total = out_v.shape[0]
+    for copy in work.shared():
+        copy.start()
+    work.head(out_v)
+
+    @pl.when(is_feed(section))
+    def _():
+        work.start_feed()
+
+        def tile(k, carry):
+            work.feed_tile(out_v, k)
+            return carry
+
+        lax.fori_loop(0, 12, tile, 0)
 
     @pl.when(section == WINDOW)
     def _():
-        attention(WINDOW)
+        work.start_attention()
+        for part in range(4):
+            work.window(out_v, part)
+        done = HEAD_ROWS + 4 * 8192
+        clear(out_v, done, total - done)
 
     @pl.when(section == LINEAR)
     def _():
-        attention(LINEAR)
-
-
-def products(normed, d_first, d_second, middle, second, grads, d_gain, total_rows):
-    count = MICRO * LEN
+        work.start_attention()
+        work.linear(out_v)
+        done = HEAD_ROWS + 20480
+        clear(out_v, done, total - done)
+
+    store = pltpu.make_async_copy(out_v, out, work.in_sem.at[0])
+    store.start()
+    store.wait()
+
+
+def products(sources, total_rows):
     return pl.pallas_call(
         products_kernel,
         out_shape=jax.ShapeDtypeStruct((total_rows, 128), BF),
         in_specs=[any_spec()] * 6 + [vmem_spec()],
         out_specs=any_spec(),
-        scratch_shapes=[
-            pltpu.VMEM((count, D), BF),
-            pltpu.VMEM((2, count, FP), BF),
-            pltpu.VMEM((2, count, FP), BF),
-            pltpu.VMEM((count, FP), BF),
-            pltpu.VMEM((count, D), BF),
-            pltpu.VMEM((D, count), BF),
-            pltpu.VMEM((512, count), BF),
-            pltpu.VMEM((512, count), BF),
-            pltpu.VMEM((FP, count), BF),
-            pltpu.VMEM((PAIR_ROWS, 128), F32),
-            pltpu.VMEM((2, PAIR_ROWS, 128), BF),
-            pltpu.SemaphoreType.DMA((5,)),
-            pltpu.SemaphoreType.DMA((2,)),
-        ],
+        scratch_shapes=[pltpu.VMEM((total_rows, 128), BF)] + product_scratch(),
         compiler_params=pltpu.CompilerParams(vmem_limit_bytes=56 * MIB),
         name="products",
-    )(normed, d_first, d_second, middle, second, grads, d_gain)
+    )(*sources)
+
+
+def reduce_kernel(chain, *refs):
+    section = lax.axis_index("section")
+    batch = lax.axis_index("batch")
+    place, core = batch // 2, lax.rem(batch, 2)
+    work = Products(refs[:7], refs[14:])
+    out, part, own, passing, total, flat, sems = refs[7:14]
+    ex_send, ex_recv, up_send, down_send, recv, out_sem = sems
+    width = own.shape[1]
+    step_rows = width - HEAD_ROWS
+    piece = width // CHUNKS
+    feed_here = is_feed(section)
+    ends = jnp.where(feed_here, chain, 2)
+    barrier = pltpu.get_barrier_semaphore()
+
+    def greet(other):
+        pl.semaphore_signal(barrier, inc=1, device_id=(section, other), device_id_type=MESH)
+
+    for copy in work.shared():
+        copy.start()
+    greet(2 * place + 1 - core)
+
+    @pl.when(place > 0)
+    def _():
+        greet(batch - 2)
+
+    @pl.when(place < chain - 1)
+    def _():
+        greet(batch + 2)
+
+    work.head(part)
+    pl.semaphore_wait(barrier, jnp.where((place > 0) & (place < chain - 1), 3, 2))
+
+    def rows_of(i):
+        return pl.ds(pl.multiple_of(i * piece, 16), piece)
+
+    def share(index, i):
+        return pl.ds(pl.multiple_of(step_rows * index + i * piece, 16), piece)
+
+    def swap(to):
+        other = 2 * to + 1 - core
+        return pltpu.make_async_remote_copy(
+            src_ref=part.at[pl.ds(pl.multiple_of(step_rows * other, 16), width), :],
+            dst_ref=own.at[to],
+            send_sem=ex_send.at[to],
+            recv_sem=ex_recv.at[to],
+            device_id=(section, 2 * place + 1 - core),
+            device_id_type=MESH,
+        )
+
+    def up_slot(at, to):
+        return to - at
+
+    def down_slot(at, to):
+        return chain - at + to
+
+    def go_up(source, to, i):
+        slot = up_slot(place + 1, to)
+        return pltpu.make_async_remote_copy(
+            src_ref=source,
+            dst_ref=passing.at[slot, rows_of(i), :],
+            send_sem=up_send.at[to - 1, i],
+            recv_sem=recv.at[slot, i],
+            device_id=(section, batch + 2),
+            device_id_type=MESH,
+        )
+
+    def go_down(source, to, i):
+        slot = down_slot(place - 1, to)
+        return pltpu.make_async_remote_copy(
+            src_ref=source,
+            dst_ref=passing.at[slot, rows_of(i), :],
+            send_sem=down_send.at[to, i],
+            recv_sem=recv.at[slot, i],
+            device_id=(section, batch - 2),
+            device_id_type=MESH,
+        )
+
+    def arrived(slot, i):
+        here = passing.at[slot, rows_of(i), :]
+        pltpu.make_async_copy(here, here, recv.at[slot, i]).wait()
+
+    def each_chunk(act):
+        def step(i, carry):
+            act(i)
+            return carry
+
+        lax.fori_loop(0, CHUNKS, step, 0)
+
+    def trade(to):
+        swap(to).start()
+        swap(to).wait()
+
+        def add(i):
+            rows = rows_of(i)
+            mine = part[share(2 * to + core, i), :].astype(F32)
+            own[to, rows, :] = (own[to, rows, :].astype(F32) + mine).astype(BF)
+
+            @pl.when((place == 0) & (to > 0))
+            def _():
+                go_up(own.at[to, rows, :], to, i).start()
+
+            @pl.when((place == chain - 1) & (to < chain - 1))
+            def _():
+                go_down(own.at[to, rows, :], to, i).start()
+
+        each_chunk(add)
+
+    @pl.when(feed_here)
+    def _():
+        work.start_feed()
+
+        def group(t, carry):
+            to = jnp.where(place < chain // 2, chain - 1 - t, t)
+
+            def tile(k, inner):
+                work.feed_tile(part, 3 * to + k)
+                return inner
+
+            lax.fori_loop(0, 3, tile, 0)
+
+            before = HEAD_ROWS + 3 * PAIR_ROWS * to
+
+            @pl.when((place < chain // 2) & ((to == 1) | (to == 2)))
+            def _():
+                first_pair = jnp.where(to == 1, 368, 240)
+                work.pairs(part, to - 1, first_pair, 16, pl.multiple_of(before - 688, 16))
+
+            @pl.when((place < chain // 2) & (to == 3))
+            def _():
+                work.down(part, 672, 16, pl.multiple_of(before - 128, 16), 128)
+
+            trade(to)
+            return carry
+
+        lax.fori_loop(0, chain, group, 0)
+
+    last_row = 4 * step_rows + HEAD_ROWS
+
+    @pl.when(section == WINDOW)
+    def _():
+        work.start_attention()
+        for index in range(3):
+            work.window(part, index)
+        trade(0)
+        work.window(part, 3)
+        done = HEAD_ROWS + 4 * 8192
+        clear(part, done, last_row - done)
+        trade(1)
+
+    @pl.when(section == LINEAR)
+    def _():
+        work.start_attention()
+        work.linear(part)
+        done = HEAD_ROWS + 20480
+        clear(part, done, last_row - done)
+        trade(0)
+        trade(1)
+
+    def pass_on(t, carry):
+        upward, downward = ends - 1 - t, t
+
+        def step(i):
+            @pl.when((place > 0) & (upward > place))
+            def _():
+                slot = up_slot(place, upward)
+                rows = rows_of(i)
+                arrived(slot, i)
+                added = passing[slot, rows, :].astype(F32) + own[upward, rows, :].astype(F32)
+                passing[slot, rows, :] = added.astype(BF)
+                go_up(passing.at[slot, rows, :], upward, i).start()
+
+            @pl.when((place < chain - 1) & (downward < place))
+            def _():
+                slot = down_slot(place, downward)
+                rows = rows_of(i)
+                arrived(slot, i)
+                added = passing[slot, rows, :].astype(F32) + own[downward, rows, :].astype(F32)
+                passing[slot, rows, :] = added.astype(BF)
+                go_down(passing.at[slot, rows, :], downward, i).start()
+
+        each_chunk(step)
+        return carry
+
+    lax.fori_loop(0, ends, pass_on, 0)
+
+    def finish(i):
+        rows = rows_of(i)
+
+        @pl.when(place < ends)
+        def _():
+            total[...] = own[place, rows, :].astype(F32)
+
+        @pl.when(place >= ends)
+        def _():
+            total[...] = jnp.zeros_like(total)
+
+        @pl.when((place > 0) & (place < ends))
+        def _():
+            arrived(0, i)
+            total[...] += passing[0, rows, :].astype(F32)
+
+        @pl.when((place < chain - 1) & (place < ends))
+        def _():
+            arrived(chain, i)
+            total[...] += passing[chain, rows, :].astype(F32)
+
+        flat[0:1, pl.ds(pl.multiple_of(i * piece * 128, 1024), piece * 128)] = total[...].reshape(1, piece * 128)
+
+    each_chunk(finish)
+    count = out.shape[1]
+    first = pl.multiple_of((8 + batch) * 128, 128)
+    store = pltpu.make_async_copy(flat.at[:, pl.ds(first, count)], out, out_sem)
+    store.start()
+
+    def drain(t, carry):
+        upward, downward = ends - 1 - t, t
+
+        def step(i):
+            @pl.when((place < chain - 1) & (upward > place))
+            def _():
+                go_up(passing.at[0, rows_of(i), :], upward, i).wait_send()
+
+            @pl.when((place > 0) & (downward < place))
+            def _():
+                go_down(passing.at[0, rows_of(i), :], downward, i).wait_send()
+
+        each_chunk(step)
+        return carry
+
+    lax.fori_loop(0, ends, drain, 0)
+    store.wait()
+
+
+def reduce_products(sources, total_rows, batches):
+    chain = batches // 2
+    step_rows = (total_rows - 8) // batches - 1
+    width = step_rows + HEAD_ROWS
+    return pl.pallas_call(
+        functools.partial(reduce_kernel, chain),
+        out_shape=jax.ShapeDtypeStruct((1, (step_rows + 1) * 128), F32),
+        in_specs=[any_spec()] * 6 + [vmem_spec()],
+        out_specs=any_spec(),
+        scratch_shapes=[
+            pltpu.VMEM((total_rows, 128), BF),
+            pltpu.VMEM((chain, width, 128), BF),
+            pltpu.VMEM((chain + 1, width, 128), BF),
+            pltpu.VMEM((width // CHUNKS, 128), F32),
+            pltpu.VMEM((1, width * 128), F32),
+            (
+                pltpu.SemaphoreType.DMA((chain,)),
+                pltpu.SemaphoreType.DMA((chain,)),
+                pltpu.SemaphoreType.DMA((chain - 1, CHUNKS)),
+                pltpu.SemaphoreType.DMA((chain - 1, CHUNKS)),
+                pltpu.SemaphoreType.DMA((chain + 1, CHUNKS)),
+                pltpu.SemaphoreType.DMA,
+            ),
+        ]
+        + product_scratch(),
+        compiler_params=pltpu.CompilerParams(
+            collective_id=2, has_side_effects=True, vmem_limit_bytes=62 * MIB
+        ),
+        name="reduce_products",
+    )(*sources)
 
 
 def document_ids(lengths):
@@ -982,9 +1248,15 @@
         cotangent, params, wide, tall, doc_col, doc_row, inputs, first, second
     )
     total_rows = params.shape[1] // 128 + 8
-    parts = products(normed, d_first, d_second, middle, second, grads, d_gain, total_rows)
-    mine = lax.psum_scatter(parts[8:].reshape(-1), "batch", scatter_dimension=0, tiled=True)
-    return acts[None], d_inputs[None], mine.astype(F32)[None]
+    sources = (normed, d_first, d_second, middle, second, grads, d_gain)
+    batches = lax.axis_size("batch")
+    if batches == 8:
+        mine = reduce_products(sources, total_rows, batches)
+    else:
+        parts = products(sources, total_rows)
+        mine = lax.psum_scatter(parts[8:].reshape(-1), "batch", scatter_dimension=0, tiled=True)
+        mine = mine.astype(F32)[None]
+    return acts[None], d_inputs[None], mine
 
 
 def solution(mesh):

time: 739 us -> 455 us (0.62)
  the two profiles are of different devices: /device:TPU:8 before, /device:TPU:10 now
where the time goes in v2:
time: 455 us; the launch traced here: 453 us
  Pallas kernels  437 us (96%)
  local copies, waits for them, and re-layouts  15.1 us (3%)
    pallas_call x1, Pallas kernels, reduce_products(): pl.pallas_call(functools.partial(reduce_kernel, chain), out_shape=jax.Sha...  199 us
    pallas_call x1, Pallas kernels, backward(): pl.pallas_call(backward_kernel, out_shape=(jax.ShapeDtypeStruct((count, D...  113 us
    pallas_call x1, Pallas kernels, prepare(): pl.pallas_call(prepare_kernel, out_shape=(jax.ShapeDtypeStruct((2, D, FP)...  73.2 us
    pallas_call x1, Pallas kernels, forward(): pl.pallas_call(forward_kernel, out_shape=(jax.ShapeDtypeStruct((count, D)...  52.1 us
    unnamed x11, local copies, waits for them, and re-layouts  13.6 us

profile of v2, /device:TPU:10, one launch (start us, length us, event | category | flops | bytes accessed | tf_op | source)
XLA Modules:
  0.0 453.5 jit_solution(15466550378998069174)
XLA Ops:
  0.6 0.9 reduce_window_sum.14
  1.5 0.1 convert_reduce_fusion
  1.6 0.6 broadcast_in_dim.15.doc_row
  2.2 0.9 copy.9.doc_col
  3.0 73.2 %prepare.1 = (bf16[2,1024,2816]{2,1,0:T(8,128)(2,1)S(1)}, bf16[2816,1024]{1,0:T(8,128)(2,1)S(1)}) custom-call(bf16[1,8455168]{1,0:T(2,128)(2,1)} %flat.5), custom_call_target="tpu_custom_call" | custom-call | tf_op jit(solution)/shard_map/prepare/pallas_call | solution.py:180
  76.2 0.0 copy-start
  76.2 4.3 copy-done
  80.6 0.0 copy-start.1
  80.6 2.4 copy-done.1
  83.0 52.1 %forward.1 = (bf16[512,1024]{1,0:T(8,128)(2,1)}, bf16[512,1024]{1,0:T(8,128)(2,1)}, bf16[512,1024]{1,0:T(8,128)(2,1)}, bf16[512,2816]{1,0:T(8,128)(2,1)}, bf16[512,2816]{1,0:T(8,128)(2,1)}) custom-call(bf16[512,1024]{1,0:T(8,128)(2,1)} %tokens.1, bf16[1,8455168]{1,0:T(2,128)(2,1)} %flat.5, bf16[2,1024,2816]{2,1,0:T(8,128)(2,1)} %copy-done, ...), custom_call_target="tpu_custom_call" | custom-call | tf_op jit(solution)/shard_map/forward/pallas_call | solution.py:450
  135.1 112.6 %backward.1 = (f32[512,1024]{1,0:T(8,128)}, bf16[512,1024]{1,0:T(8,128)(2,1)}, bf16[512,2816]{1,0:T(8,128)(2,1)}, bf16[512,2816]{1,0:T(8,128)(2,1)}, bf16[512,2816]{1,0:T(8,128)(2,1)}, /*index=5*/f32[8,1024]{1,0:T(8,128)}) custom-call(bf16[512,1024]{1,0:T(8,128)(2,1)} %cotangent.1, bf16[1,8455168]{1,0:T(2,128)(2,1)} %flat.5, bf16[2,1024,2816]{2,1,0:T(8,128)(2,1)} %copy-done, ...), custom_call_target="tpu_custom_call" | custom-call | tf_op jit(solution)/shard_map/backward/pallas_call | solution.py:703
  247.7 0.0 copy-start.3
  247.7 198.9 %reduce_products.1 = f32[1,1056896]{1,0:T(1,128)} custom-call(bf16[512,1024]{1,0:T(8,128)(2,1)} %get-tuple-element.23.refs_0_, bf16[512,2816]{1,0:T(8,128)(2,1)} %get-tuple-element.24.refs_1_, bf16[512,2816]{1,0:T(8,128)(2,1)} %get-tuple-element.25.refs_2_, bf16[512,2816]{1,0:T(8,128)(2,1)} %get-tuple-element.26.refs_3_, ...), custom_call_target="tpu_custom_call" | custom-call | tf_op jit(solution)/shard_map/reduce_products/pallas_call | solution.py:1208
  446.6 0.0 copy-done.3
  446.6 0.0 copy-start.2
  446.6 1.0 copy.14
  447.6 3.8 copy.15
  451.4 0.0 copy-done.2
  451.4 2.0 copy.16
Async XLA Ops:
  76.2 4.4 copy-start
  80.6 2.4 copy-start.1
  247.7 198.9 %copy-start.3 = (bf16[512,1024]{1,0:T(8,128)(2,1)S(1)}, bf16[512,1024]{1,0:T(8,128)(2,1)}, u32[]{:S(2)}) copy-start(bf16[512,1024]{1,0:T(8,128)(2,1)} %get-tuple-element.18) | copy-start | bytes 3145732
  446.6 4.8 %copy-start.2 = (f32[1,1056896]{1,0:T(1,128)S(1)}, f32[1,1056896]{1,0:T(1,128)}, u32[]{:S(2)}) copy-start(f32[1,1056896]{1,0:T(1,128)} %reduce_products.1) | copy-start | bytes 12682756

commit v3 on v2

v3 whole, which is shorter than its diff:
```python
import functools
import math

import jax
import jax.numpy as jnp
from jax import lax
from jax.experimental import pallas as pl
from jax.experimental.pallas import tpu as pltpu
from jax.sharding import PartitionSpec as P

D = 1024
FF = 2752
FP = 2816
HEADS = 16
FEAT = 16
WIN = 64
MICRO = 2
LEN = 256
EPSILON = 1e-06
SCALE = 1.0 / math.sqrt(D)
LINEAR, FEED, WINDOW, FEED2 = 0, 1, 2, 3
MIB = 2**20
MESH = pl.DeviceIdType.MESH
BF = jnp.bfloat16
F32 = jnp.float32


def any_spec():
    return pl.BlockSpec(memory_space=pl.ANY)


def vmem_spec():
    return pl.BlockSpec(memory_space=pltpu.VMEM)


def dot(left, right):
    return jnp.dot(left, right, preferred_element_type=F32)


def dot_t(left, right):
    return lax.dot_general(left, right, (((1,), (1,)), ((), ())), preferred_element_type=F32)


def dot_0(left, right):
    return lax.dot_general(left, right, (((0,), (0,)), ((), ())), preferred_element_type=F32)


def is_feed(section):
    return (section == FEED) | (section == FEED2)


PAIR_STEP = 32 * FF
ROW_STEP = 64 * D
AHEAD = 8


def prepare(section, flat, wide_v, tall_v, chunk, blocks, woven, load_sem):
    def run(steps, count, first, work):
        def load(i):
            slot = lax.rem(i, AHEAD)
            return pltpu.make_async_copy(
                flat.at[:, pl.ds(pl.multiple_of(first + i * count, 1024), count)],
                chunk.at[slot, :, pl.ds(0, count)],
                load_sem.at[slot],
            )

        def start(i, carry):
            load(i).start()
            return carry

        lax.fori_loop(0, AHEAD, start, 0)

        def step(i, carry):
            load(i).wait()
            rows = count // 128
            blocks[pl.ds(0, rows), :] = chunk[lax.rem(i, AHEAD), :, pl.ds(0, count)].astype(F32).reshape(rows, 128)
            work(i)

            @pl.when(i + AHEAD < steps)
            def _():
                load(i + AHEAD).start()

            return carry

        lax.fori_loop(0, steps, step, 0)

    def rows_of(index, count):
        return pl.ds(pl.multiple_of(index * count, count), count)

    def pair_work(i):
        low_half = lax.broadcasted_iota(jnp.int32, (16, 128), 1) < 64
        rolled = pltpu.roll(blocks[pl.ds(21, 16, stride=43), :], 64, 1)
        for c in range(22):
            even = blocks[pl.ds(c, 16, stride=43), :]
            if c == 21:
                even = jnp.where(low_half, even, 0.0)
                odd = jnp.where(low_half, rolled, 0.0)
            else:
                after = pltpu.roll(blocks[pl.ds(22 + c, 16, stride=43), :], 64, 1)
                odd = jnp.where(low_half, rolled, after)
                rolled = after
            woven[c, pl.ds(0, 16, stride=2), :] = even
            woven[c, pl.ds(1, 16, stride=2), :] = odd
        rows = rows_of(lax.rem(i, 32), 32)
        for c in range(22):
            wide_v[i // 32, rows, pl.ds(128 * c, 128)] = woven[c].astype(BF)

    def row_work(target, rows, first_col):
        for c in range(8):
            target[rows, pl.ds(first_col + 128 * c, 128)] = blocks[pl.ds(c, 64, stride=8), :].astype(BF)

    def square(i, first, target, first_col):
        @pl.when((i >= first) & (i < first + 16))
        def _():
            row_work(target, rows_of(i - first, 64), first_col)

    @pl.when(is_feed(section))
    def _():
        run(64, PAIR_STEP, D, pair_work)
        run(43, ROW_STEP, D + 2 * D * FF, lambda i: row_work(tall_v, rows_of(i, 64), 0))
        tall_v[pl.ds(FF, FP - FF), :] = jnp.zeros((FP - FF, D), BF)

    @pl.when(section == WINDOW)
    def _():
        def work(i):
            square(i, 0, wide_v.at[0], 0)
            square(i, 16, wide_v.at[0], D)
            square(i, 32, wide_v.at[1], 0)
            square(i, 48, tall_v, 0)

        run(64, ROW_STEP, D, work)

    @pl.when(section == LINEAR)
    def _():
        def work(i):
            for part in range(2):

                @pl.when(i // 4 == part)
                def _(part=part):
                    rows = rows_of(i - 4 * part, 256)
                    for c in range(2):
                        cols = pl.ds(part * HEADS * FEAT + 128 * c, 128)
                        wide_v[0, rows, cols] = blocks[pl.ds(c, 256, stride=2), :].astype(BF)

            square(i, 8, wide_v.at[1], 0)
            square(i, 24, tall_v, 0)

        run(40, ROW_STEP, D, work)


ROWS = 128
CHUNKS_OF = LEN // ROWS


def lanes_of_head(kind, block, half):
    lanes = lax.broadcasted_iota(jnp.int32, (1, 128), 1)
    if kind == WINDOW:
        return lanes // 64 == half
    return lanes // FEAT == lax.rem(2 * block + half, 8)


def lanes_of_value(half):
    return lax.broadcasted_iota(jnp.int32, (1, 128), 1) // 64 == half


def only(mask, values):
    return jnp.where(mask, values, jnp.zeros_like(values))


def both(masks, values):
    return jnp.concatenate([only(masks[0], values), only(masks[1], values)], axis=0)


def merge(masks, stacked):
    return only(masks[0], stacked[:ROWS]) + only(masks[1], stacked[ROWS:])


def block_of(index, first=0):
    return pl.ds(pl.multiple_of(first + index * 128, 128), 128)


def query_index(kind, block):
    return block if kind == WINDOW else block // 4


def low_width(kind):
    return D if kind == WINDOW else HEADS * FEAT


def mask_of(kind, doc_col, doc_row, first_row):
    shape = (doc_col.shape[0], doc_row.shape[1])
    rows = lax.broadcasted_iota(jnp.int32, shape, 0) + first_row
    cols = lax.broadcasted_iota(jnp.int32, shape, 1)
    mask = (doc_col == doc_row) & (cols <= rows)
    if kind == WINDOW:
        mask = mask & (rows - cols < WIN)
    return mask.astype(F32)


def root_of(kind):
    return 1.0 / math.sqrt(D // HEADS if kind == WINDOW else FEAT)


def out_scale(kind):
    return {LINEAR: 8.0, WINDOW: 4.0, FEED: 1.0}[kind] * SCALE


def train_kernel(
    tokens, cotangent, flat, doc_col, doc_row,
    acts, d_inputs, normed, middle, d_first, d_second, grads, d_gain,
    wide_v, tall_v, gain_v, z_v, h_v, x_v, g_v, dz_v, first_v, second_v, mid_v, dh_v,
    raised_v, slope_v, inverse_v, mask_v, dy_v, dq_v, dk_v, dv_v, chunk, blocks, woven,
    load_sem, gain_sem, in_sem, act_sem, out_sem, on_send, on_recv, back_send, back_recv,
):
    section = lax.axis_index("section")
    batch = lax.axis_index("batch")
    last = lax.axis_size("section") - 1
    barrier = pltpu.get_barrier_semaphore()

    @pl.when(section > 0)
    def _():
        pl.semaphore_signal(barrier, inc=1, device_id=(section - 1, batch), device_id_type=MESH)

    @pl.when(section < last)
    def _():
        pl.semaphore_signal(barrier, inc=1, device_id=(section + 1, batch), device_id_type=MESH)

    gain_copy = pltpu.make_async_copy(flat.at[:, pl.ds(0, D)], gain_v, gain_sem)
    gain_copy.start()
    token_copy = pltpu.make_async_copy(tokens, z_v, in_sem.at[0])
    tangent_copy = pltpu.make_async_copy(cotangent, g_v, in_sem.at[1])

    @pl.when(section == 0)
    def _():
        token_copy.start()

    @pl.when(section == last)
    def _():
        tangent_copy.start()

    prepare(section, flat, wide_v, tall_v, chunk, blocks, woven, load_sem)
    gain_copy.wait()
    gain = 1.0 + gain_v[...].astype(F32) / 8.0
    d_gain[...] = jnp.zeros_like(d_gain)

    @pl.when(section == 0)
    def _():
        token_copy.wait()

    pl.semaphore_wait(barrier, jnp.where((section > 0) & (section < last), 2, 1))

    def rows_at(step):
        return pl.ds(pl.multiple_of(step * ROWS, ROWS), ROWS)

    def hand_on(step):
        rows = rows_at(step)
        return pltpu.make_async_remote_copy(
            src_ref=x_v.at[rows, :],
            dst_ref=z_v.at[rows, :],
            send_sem=on_send.at[step],
            recv_sem=on_recv.at[step],
            device_id=(section + 1, batch),
            device_id_type=MESH,
        )

    def hand_back(step):
        rows = rows_at(step)
        return pltpu.make_async_remote_copy(
            src_ref=x_v.at[rows, :],
            dst_ref=g_v.at[rows, :],
            send_sem=back_send.at[step],
            recv_sem=back_recv.at[step],
            device_id=(section - 1, batch),
            device_id_type=MESH,
        )

    def forward_outs(step):
        rows = rows_at(step)
        return [
            pltpu.make_async_copy(x_v.at[rows, :], acts.at[rows, :], act_sem.at[0, step]),
            pltpu.make_async_copy(h_v.at[rows, :], normed.at[rows, :], act_sem.at[1, step]),
            pltpu.make_async_copy(mid_v.at[rows, :], middle.at[rows, :], act_sem.at[2, step]),
        ]

    def backward_outs(step):
        rows = rows_at(step)
        return [
            pltpu.make_async_copy(dz_v.at[rows, :], d_inputs.at[rows, :], out_sem.at[0, step]),
            pltpu.make_async_copy(g_v.at[rows, :], grads.at[rows, :], out_sem.at[1, step]),
            pltpu.make_async_copy(first_v.at[rows, :], d_first.at[rows, :], out_sem.at[2, step]),
            pltpu.make_async_copy(second_v.at[rows, :], d_second.at[rows, :], out_sem.at[3, step]),
        ]


    def forward_step(step, branch):
        rows = rows_at(step)

        @pl.when(section > 0)
        def _():
            hand_on(step).wait_recv()

        z = z_v[rows, :].astype(F32)
        scaled = lax.rsqrt(jnp.mean(z * z, axis=1, keepdims=True) + EPSILON)
        h_v[rows, :] = (z * scaled * gain).astype(BF)
        x_v[rows, :] = (z_v[rows, :].astype(F32) + branch(rows)).astype(BF)

        @pl.when(section < last)
        def _():
            hand_on(step).start()

        for copy in forward_outs(step):
            copy.start()

    def backward_step(step, branch):
        rows = rows_at(step)

        @pl.when(section < last)
        def _():
            hand_back(step).wait_recv()

        branch(rows)
        z = z_v[rows, :].astype(F32)
        scaled = lax.rsqrt(jnp.mean(z * z, axis=1, keepdims=True) + EPSILON)
        unit = z * scaled
        d_normed = dh_v[...]
        d_gain[0:1, :] += jnp.sum(d_normed * unit, axis=0, keepdims=True) * 0.125
        d_unit = d_normed * gain
        d_z = scaled * (d_unit - unit * jnp.mean(d_unit * unit, axis=1, keepdims=True))
        d_z += g_v[rows, :].astype(F32)
        dz_v[rows, :] = d_z
        x_v[rows, :] = d_z.astype(BF)

        @pl.when(section > 0)
        def _():
            hand_back(step).start()

        for copy in backward_outs(step):
            copy.start()

    def feed_forward(rows):
        half = FP // 2
        for part in range(2):
            cols = pl.ds(part * half, half)
            gate = dot(h_v[rows, :], wide_v[0, :, cols]) * SCALE
            up = dot(h_v[rows, :], wide_v[1, :, cols]) * SCALE
            sig = 1.0 / (1.0 + jnp.exp(-gate))
            silu = gate * sig
            first_v[rows, cols] = (up * (sig + silu * (1.0 - sig))).astype(BF)
            second_v[rows, cols] = silu.astype(BF)
            mid_v[rows, cols] = (silu * up).astype(BF)
        return dot(mid_v[rows, :], tall_v[...]) * SCALE

    def feed_backward(rows):
        half = FP // 2
        for part in range(2):
            cols = pl.ds(part * half, half)
            d_mid = dot_t(g_v[rows, :], tall_v[cols, :]) * SCALE
            first_v[rows, cols] = (d_mid * first_v[rows, cols].astype(F32)).astype(BF)
            second_v[rows, cols] = (d_mid * second_v[rows, cols].astype(F32)).astype(BF)
        total = dot_t(first_v[rows, :], wide_v[0]) + dot_t(second_v[rows, :], wide_v[1])
        dh_v[...] = total * SCALE

    def attend_forward(kind, micro, part, rows):
        width = low_width(kind)
        span = ROWS * (part + 1)
        keys_at = pl.ds(pl.multiple_of(micro * LEN, LEN), span)
        step = micro * CHUNKS_OF + part
        first_v[rows, pl.ds(0, 2 * width)] = (dot(h_v[rows, :], wide_v[0, :, pl.ds(0, 2 * width)]) * SCALE).astype(BF)
        second_v[rows, pl.ds(0, D)] = (dot(h_v[rows, :], wide_v[1, :, pl.ds(0, D)]) * SCALE).astype(BF)
        cols = pl.ds(0, span)
        mask_v[:, cols] = mask_of(
            kind, doc_col[micro, pl.ds(part * ROWS, ROWS), :], doc_row[micro, :, pl.ds(0, span)], part * ROWS
        )

        def block(t, carry):
            index = query_index(kind, t)
            queries = first_v[rows, block_of(index)]
            keys = first_v[keys_at, block_of(index, width)]
            values = second_v[keys_at, block_of(t)]
            heads = [lanes_of_head(kind, t, half) for half in range(2)]
            scores = (dot_t(both(heads, queries), keys) * root_of(kind)).reshape(2, ROWS, span)
            mask = mask_v[:, cols]
            if kind == WINDOW:
                kept = jnp.where((mask > 0.0)[None], scores, -1e30)
                raised = jnp.exp(kept - jnp.max(kept, axis=2, keepdims=True))
            else:
                slope = mask[None] * (1.0 + scores)
                slope_v[step, t, :, cols] = slope.astype(BF).reshape(2 * ROWS, span)
                raised = 0.5 * (mask[None] + slope * slope)
            raised = raised.astype(BF).reshape(2 * ROWS, span)
            raised_v[step, t, :, cols] = raised
            summed = dot(raised, jnp.concatenate([values, jnp.ones((span, 128), BF)], axis=1))
            inverse = 1.0 / summed[:, 128:]
            sides = [lanes_of_value(half) for half in range(2)]
            mid_v[rows, block_of(t)] = merge(sides, summed[:, :128] * inverse).astype(BF)
            inverse_v[rows, block_of(t)] = merge(sides, inverse)
            return carry

        lax.fori_loop(0, 8, block, 0, unroll=UNROLL)
        return dot(mid_v[rows, pl.ds(0, D)], tall_v[pl.ds(0, D), :]) * out_scale(kind)

    def attend_backward(kind, micro, part, rows):
        width = low_width(kind)
        span = ROWS * (part + 1)
        keys_at = pl.ds(pl.multiple_of(micro * LEN, LEN), span)
        own = pl.ds(0, span)
        step = micro * CHUNKS_OF + part
        d_mixed = dot_t(g_v[rows, :], tall_v[pl.ds(0, D), :]) * out_scale(kind)
        dy_v[...] = (d_mixed * inverse_v[rows, :]).astype(BF)
        if part == CHUNKS_OF - 1:
            dk_v[...] = jnp.zeros_like(dk_v)
            dv_v[...] = jnp.zeros_like(dv_v)
        if kind == LINEAR:
            dq_v[...] = jnp.zeros_like(dq_v)

        def block(t, carry):
            index = query_index(kind, t)
            queries = first_v[rows, block_of(index)]
            keys = first_v[keys_at, block_of(index, width)]
            values = second_v[keys_at, block_of(t)]
            heads = [lanes_of_head(kind, t, half) for half in range(2)]
            sides = [lanes_of_value(half) for half in range(2)]
            d_mixed = both(sides, dy_v[:, block_of(t)])
            mixed = mid_v[rows, block_of(t)].astype(F32)
            shift = jnp.sum(d_mixed.astype(F32) * jnp.concatenate([mixed, mixed], axis=0), axis=1, keepdims=True)
            d_weights = dot_t(d_mixed, values) - shift
            raised = raised_v[step, t, :, own]
            slope = raised if kind == WINDOW else slope_v[step, t, :, own]
            d_scores = (slope.astype(F32) * d_weights).astype(BF)
            dv_v[own, block_of(t)] += dot_0(raised, d_mixed)
            d_queries = merge(heads, dot(d_scores, keys)) * root_of(kind)
            dk_v[own, block_of(index)] += dot_0(d_scores, both(heads, queries)) * root_of(kind)
            if kind == WINDOW:
                dq_v[:, block_of(t)] = d_queries
            else:
                dq_v[:, block_of(index)] += d_queries
            return carry

        lax.fori_loop(0, 8, block, 0, unroll=UNROLL)
        done = pl.ds(part * ROWS, ROWS)
        first_v[rows, pl.ds(0, width)] = dq_v[:, pl.ds(0, width)].astype(BF)
        first_v[rows, pl.ds(width, width)] = dk_v[done, pl.ds(0, width)].astype(BF)
        second_v[rows, pl.ds(0, D)] = dv_v[done, :].astype(BF)
        total = dot_t(first_v[rows, pl.ds(0, 2 * width)], wide_v[0, :, pl.ds(0, 2 * width)])
        total += dot_t(second_v[rows, pl.ds(0, D)], wide_v[1, :, pl.ds(0, D)])
        dh_v[...] = total * SCALE

    steps = MICRO * CHUNKS_OF

    @pl.when(is_feed(section))
    def _():
        def forward(step, carry):
            forward_step(step, feed_forward)
            return carry

        lax.fori_loop(0, steps, forward, 0)

    for kind in (WINDOW, LINEAR):

        @pl.when(section == kind)
        def _(kind=kind):
            def forward(micro, carry):
                for part in range(CHUNKS_OF):
                    forward_step(
                        micro * CHUNKS_OF + part, functools.partial(attend_forward, kind, micro, part)
                    )
                return carry

            lax.fori_loop(0, MICRO, forward, 0)

    def settle(step, carry):
        @pl.when(section < last)
        def _():
            hand_on(step).wait_send()

        for copy in forward_outs(step):
            copy.wait()
        return carry

    lax.fori_loop(0, steps, settle, 0)

    @pl.when(section == last)
    def _():
        tangent_copy.wait()

    @pl.when(is_feed(section))
    def _():
        def backward(step, carry):
            micro, part = step // CHUNKS_OF, CHUNKS_OF - 1 - lax.rem(step, CHUNKS_OF)
            backward_step(micro * CHUNKS_OF + part, feed_backward)
            return carry

        lax.fori_loop(0, steps, backward, 0)

    for kind in (WINDOW, LINEAR):

        @pl.when(section == kind)
        def _(kind=kind):
            def backward(micro, carry):
                for part in reversed(range(CHUNKS_OF)):
                    backward_step(
                        micro * CHUNKS_OF + part, functools.partial(attend_backward, kind, micro, part)
                    )
                return carry

            lax.fori_loop(0, MICRO, backward, 0)

    def finish(step, carry):
        @pl.when(section > 0)
        def _():
            hand_back(step).wait_send()

        for copy in backward_outs(step):
            copy.wait()
        return carry

    lax.fori_loop(0, steps, finish, 0)


UNROLL = 2


def train(tokens, cotangent, flat, doc_col, doc_row):
    count = MICRO * LEN
    steps = MICRO * CHUNKS_OF
    return pl.pallas_call(
        train_kernel,
        out_shape=(
            jax.ShapeDtypeStruct((count, D), BF),
            jax.ShapeDtypeStruct((count, D), F32),
            jax.ShapeDtypeStruct((count, D), BF),
            jax.ShapeDtypeStruct((count, FP), BF),
            jax.ShapeDtypeStruct((count, FP), BF),
            jax.ShapeDtypeStruct((count, FP), BF),
            jax.ShapeDtypeStruct((count, D), BF),
            jax.ShapeDtypeStruct((8, D), F32),
        ),
        in_specs=[any_spec()] * 3 + [vmem_spec()] * 2,
        out_specs=(any_spec(),) * 7 + (vmem_spec(),),
        scratch_shapes=[
            pltpu.VMEM((2, D, FP), BF),
            pltpu.VMEM((FP, D), BF),
            pltpu.VMEM((1, D), BF),
            pltpu.VMEM((count, D), BF),
            pltpu.VMEM((count, D), BF),
            pltpu.VMEM((count, D), BF),
            pltpu.VMEM((count, D), BF),
            pltpu.VMEM((count, D), F32),
            pltpu.VMEM((count, FP), BF),
            pltpu.VMEM((count, FP), BF),
            pltpu.VMEM((count, FP), BF),
            pltpu.VMEM((ROWS, D), F32),
            pltpu.VMEM((steps, 8, 2 * ROWS, LEN), BF),
            pltpu.VMEM((steps, 8, 2 * ROWS, LEN), BF),
            pltpu.VMEM((count, D), F32),
            pltpu.VMEM((ROWS, LEN), F32),
            pltpu.VMEM((ROWS, D), BF),
            pltpu.VMEM((ROWS, D), F32),
            pltpu.VMEM((LEN, D), F32),
            pltpu.VMEM((LEN, D), F32),
            pltpu.VMEM((AHEAD, 1, PAIR_STEP), BF),
            pltpu.VMEM((PAIR_STEP // 128, 128), F32),
            pltpu.VMEM((22, 32, 128), F32),
            pltpu.SemaphoreType.DMA((AHEAD,)),
            pltpu.SemaphoreType.DMA,
            pltpu.SemaphoreType.DMA((2,)),
            pltpu.SemaphoreType.DMA((3, steps)),
            pltpu.SemaphoreType.DMA((4, steps)),
            pltpu.SemaphoreType.DMA((steps,)),
            pltpu.SemaphoreType.DMA((steps,)),
            pltpu.SemaphoreType.DMA((steps,)),
            pltpu.SemaphoreType.DMA((steps,)),
        ],
        compiler_params=pltpu.CompilerParams(
            collective_id=0, has_side_effects=True, vmem_limit_bytes=62 * MIB
        ),
        name="train",
    )(tokens, cotangent, flat, doc_col, doc_row)


HEAD_ROWS = 16
PAIR_ROWS = 128 * 43
CHUNKS = 11


def flip(source, first, width, target):
    def piece(t, carry):
        cols = pl.ds(pl.multiple_of(t * 128, 128), 128)
        rows = pl.ds(pl.multiple_of(first + t * 128, 128), 128)
        target[rows, :] = source[:, cols].astype(F32).T.astype(target.dtype)
        return carry

    lax.fori_loop(0, width // 128, piece, 0)


class Products:
    def __init__(self, sources, scratch):
        self.normed, self.d_first, self.d_second, self.middle, self.grads, self.d_gain = sources
        self.h_v, self.d_v, self.m_v, self.g_v, self.turned, self.m_turned, self.stage, self.in_sem = scratch

    def fetch(self, source, target, index):
        return pltpu.make_async_copy(source, target, self.in_sem.at[index])

    def shared(self):
        return [
            self.fetch(self.normed, self.h_v, 0),
            self.fetch(self.grads, self.g_v, 1),
            self.fetch(self.d_first, self.d_v.at[0], 2),
            self.fetch(self.d_second, self.d_v.at[1], 3),
        ]

    def middle_half(self, part):
        half = FP // 2
        return self.fetch(self.middle.at[:, pl.ds(part * half, half)], self.m_v, 4)

    def mixed(self):
        return self.fetch(self.middle.at[:, pl.ds(0, D)], self.m_v.at[:, pl.ds(0, D)], 4)

    def head(self, out):
        stage = self.stage
        stage[pl.ds(0, 8), :] = jnp.zeros((8, 128), F32)
        stage[pl.ds(8, 8), :] = self.d_gain[0:1, :].reshape(8, 128)
        out[pl.ds(0, 16), :] = stage[pl.ds(0, 16), :].astype(BF)

    def cut(self, out, first_row, rows, piece):
        def step(j, carry):
            source = pl.ds(pl.multiple_of(j * piece, 16), piece)
            target = pl.ds(pl.multiple_of(first_row + j * piece, 16), piece)
            out[target, :] = self.stage[source, :].astype(BF)
            return carry

        lax.fori_loop(0, rows // piece, step, 0)

    def start_feed(self):
        self.middle_half(0).start()
        for copy in self.shared():
            copy.wait()
        stage = self.stage

        def halves(t, carry):
            cols = pl.ds(pl.multiple_of(t * 128, 128), 128)
            stage[pl.ds(0, 512), :] = self.h_v[:, cols].astype(F32)
            for part in range(4):
                stage[pl.ds(512 + 128 * part, 128), :] = stage[pl.ds(128 * part, 128), :].T
            for part in range(4):
                for odd in range(2):
                    rows = pl.ds(pl.multiple_of(512 * odd + t * 64, 64), 64)
                    piece = stage[pl.ds(512 + 128 * part + odd, 64, stride=2), :]
                    self.turned[rows, pl.ds(128 * part, 128)] = piece.astype(BF)
            return carry

        lax.fori_loop(0, 8, halves, 0)
        half = FP // 2
        for part in range(2):
            self.middle_half(part).wait()
            flip(self.m_v, part * half, half, self.m_turned)
            if part == 0:
                self.middle_half(1).start()

    def pairs(self, out, which, first_pair, count, first_row):
        stage = self.stage
        half = FP // 2
        low_half = lax.broadcasted_iota(jnp.int32, (count, 128), 1) < 64
        even = self.turned[pl.ds(pl.multiple_of(first_pair, 16), count), :]
        odd = self.turned[pl.ds(pl.multiple_of(512 + first_pair, 16), count), :]
        for part in range(2):
            piece = dot(even, self.d_v[which, :, pl.ds(part * half, half)]) * SCALE
            for c in range(11):
                stage[pl.ds(11 * part + c, count, stride=43), :] = piece[:, 128 * c : 128 * c + 128]
        before = stage[pl.ds(21, count, stride=43), :]
        for part in range(2):
            piece = dot(odd, self.d_v[which, :, pl.ds(part * half, half)]) * SCALE
            for c in range(11):
                here = pltpu.roll(piece[:, 128 * c : 128 * c + 128], 64, 1)
                stage[pl.ds(21 + 11 * part + c, count, stride=43), :] = jnp.where(low_half, before, here)
                before = here
        self.cut(out, first_row, 43 * count, 688)

    def tall(self, out, left, right, stride, rows, first_row, scale, piece):
        product = dot(left, right) * scale
        for c in range(stride):
            self.stage[pl.ds(c, rows, stride=stride), :] = product[:, 128 * c : 128 * c + 128]
        self.cut(out, first_row, rows * stride, piece)

    def down(self, out, first_channel, rows, first_row, piece):
        left = self.m_turned[pl.ds(pl.multiple_of(first_channel, 16), rows), :]
        self.tall(out, left, self.g_v[...], 8, rows, first_row, SCALE, piece)

    def feed_tile(self, out, k):
        first_row = pl.multiple_of(HEAD_ROWS + k * PAIR_ROWS, 16)

        @pl.when(k < 8)
        def _():
            self.pairs(out, k // 4, lax.rem(k, 4) * 128, 128, first_row)

        @pl.when(k >= 8)
        def _():
            self.down(out, (k - 8) * 688, 688, first_row, 688)

    def start_attention(self):
        self.mixed().start()
        for copy in self.shared():
            copy.wait()
        flip(self.h_v, 0, D, self.turned)
        self.mixed().wait()
        flip(self.m_v, 0, D, self.m_turned)

    def square(self, out, left, right, first_row, scale):
        def step(i, carry):
            rows = pl.ds(pl.multiple_of(i * 512, 512), 512)
            self.tall(out, left[rows, :], right(), 8, 512, pl.multiple_of(first_row + i * 4096, 16), scale, 512)
            return carry

        lax.fori_loop(0, 2, step, 0)

    def window(self, out, part):
        first_row = HEAD_ROWS + part * 8192
        if part < 3:
            cols = pl.ds(D if part == 1 else 0, D)
            self.square(out, self.turned, lambda: self.d_v[part // 2, :, cols], first_row, SCALE)
        else:
            self.square(out, self.m_turned, lambda: self.g_v[...], first_row, out_scale(WINDOW))

    def linear(self, out):
        width = HEADS * FEAT
        for part in range(2):
            right = self.d_v[0, :, pl.ds(part * width, width)]
            self.tall(out, self.turned[...], right, 2, D, HEAD_ROWS + part * 2048, SCALE, 512)
        self.square(out, self.turned, lambda: self.d_v[1, :, pl.ds(0, D)], HEAD_ROWS + 4096, SCALE)
        self.square(out, self.m_turned, lambda: self.g_v[...], HEAD_ROWS + 12288, out_scale(LINEAR))


def product_scratch():
    count = MICRO * LEN
    return [
        pltpu.VMEM((count, D), BF),
        pltpu.VMEM((2, count, FP), BF),
        pltpu.VMEM((count, FP // 2), BF),
        pltpu.VMEM((count, D), BF),
        pltpu.VMEM((D, count), BF),
        pltpu.VMEM((FP, count), BF),
        pltpu.VMEM((PAIR_ROWS, 128), F32),
        pltpu.SemaphoreType.DMA((5,)),
    ]


def clear(out, first_row, rows):
    def step(i, carry):
        out[pl.ds(pl.multiple_of(first_row + i * 128, 16), 128), :] = jnp.zeros((128, 128), BF)
        return carry

    lax.fori_loop(0, rows // 128, step, 0)
    if rows % 128:
        out[pl.ds(first_row + rows // 128 * 128, rows % 128), :] = jnp.zeros((rows % 128, 128), BF)


def products_kernel(*refs):
    section = lax.axis_index("section")
    work = Products(refs[:6], refs[8:])
    out, out_v = refs[6:8]
    total = out_v.shape[0]
    for copy in work.shared():
        copy.start()
    work.head(out_v)

    @pl.when(is_feed(section))
    def _():
        work.start_feed()

        def tile(k, carry):
            work.feed_tile(out_v, k)
            return carry

        lax.fori_loop(0, 12, tile, 0)

    @pl.when(section == WINDOW)
    def _():
        work.start_attention()
        for part in range(4):
            work.window(out_v, part)
        done = HEAD_ROWS + 4 * 8192
        clear(out_v, done, total - done)

    @pl.when(section == LINEAR)
    def _():
        work.start_attention()
        work.linear(out_v)
        done = HEAD_ROWS + 20480
        clear(out_v, done, total - done)

    store = pltpu.make_async_copy(out_v, out, work.in_sem.at[0])
    store.start()
    store.wait()


def products(sources, total_rows):
    return pl.pallas_call(
        products_kernel,
        out_shape=jax.ShapeDtypeStruct((total_rows, 128), BF),
        in_specs=[any_spec()] * 5 + [vmem_spec()],
        out_specs=any_spec(),
        scratch_shapes=[pltpu.VMEM((total_rows, 128), BF)] + product_scratch(),
        compiler_params=pltpu.CompilerParams(vmem_limit_bytes=56 * MIB),
        name="products",
    )(*sources)


def reduce_kernel(chain, *refs):
    section = lax.axis_index("section")
    batch = lax.axis_index("batch")
    place, core = batch // 2, lax.rem(batch, 2)
    work = Products(refs[:6], refs[13:])
    out, part, own, passing, total, flat, sems = refs[6:13]
    ex_send, ex_recv, up_send, down_send, recv, out_sem = sems
    width = own.shape[1]
    step_rows = width - HEAD_ROWS
    piece = width // CHUNKS
    feed_here = is_feed(section)
    ends = jnp.where(feed_here, chain, 2)
    barrier = pltpu.get_barrier_semaphore()

    def greet(other):
        pl.semaphore_signal(barrier, inc=1, device_id=(section, other), device_id_type=MESH)

    for copy in work.shared():
        copy.start()
    greet(2 * place + 1 - core)

    @pl.when(place > 0)
    def _():
        greet(batch - 2)

    @pl.when(place < chain - 1)
    def _():
        greet(batch + 2)

    work.head(part)
    pl.semaphore_wait(barrier, jnp.where((place > 0) & (place < chain - 1), 3, 2))

    def rows_of(i):
        return pl.ds(pl.multiple_of(i * piece, 16), piece)

    def share(index, i):
        return pl.ds(pl.multiple_of(step_rows * index + i * piece, 16), piece)

    def swap(to):
        other = 2 * to + 1 - core
        return pltpu.make_async_remote_copy(
            src_ref=part.at[pl.ds(pl.multiple_of(step_rows * other, 16), width), :],
            dst_ref=own.at[to],
            send_sem=ex_send.at[to],
            recv_sem=ex_recv.at[to],
            device_id=(section, 2 * place + 1 - core),
            device_id_type=MESH,
        )

    def up_slot(at, to):
        return to - at

    def down_slot(at, to):
        return chain - at + to

    def go_up(source, to, i):
        slot = up_slot(place + 1, to)
        return pltpu.make_async_remote_copy(
            src_ref=source,
            dst_ref=passing.at[slot, rows_of(i), :],
            send_sem=up_send.at[to - 1, i],
            recv_sem=recv.at[slot, i],
            device_id=(section, batch + 2),
            device_id_type=MESH,
        )

    def go_down(source, to, i):
        slot = down_slot(place - 1, to)
        return pltpu.make_async_remote_copy(
            src_ref=source,
            dst_ref=passing.at[slot, rows_of(i), :],
            send_sem=down_send.at[to, i],
            recv_sem=recv.at[slot, i],
            device_id=(section, batch - 2),
            device_id_type=MESH,
        )

    def arrived(slot, i):
        here = passing.at[slot, rows_of(i), :]
        pltpu.make_async_copy(here, here, recv.at[slot, i]).wait()

    def each_chunk(act):
        def step(i, carry):
            act(i)
            return carry

        lax.fori_loop(0, CHUNKS, step, 0)

    def trade(to):
        swap(to).start()
        swap(to).wait()

        def add(i):
            rows = rows_of(i)
            mine = part[share(2 * to + core, i), :].astype(F32)
            own[to, rows, :] = (own[to, rows, :].astype(F32) + mine).astype(BF)

            @pl.when((place == 0) & (to > 0))
            def _():
                go_up(own.at[to, rows, :], to, i).start()

            @pl.when((place == chain - 1) & (to < chain - 1))
            def _():
                go_down(own.at[to, rows, :], to, i).start()

        each_chunk(add)

    @pl.when(feed_here)
    def _():
        work.start_feed()

        def group(t, carry):
            to = jnp.where(place < chain // 2, chain - 1 - t, t)

            def tile(k, inner):
                work.feed_tile(part, 3 * to + k)
                return inner

            lax.fori_loop(0, 3, tile, 0)

            before = HEAD_ROWS + 3 * PAIR_ROWS * to

            @pl.when((place < chain // 2) & ((to == 1) | (to == 2)))
            def _():
                first_pair = jnp.where(to == 1, 368, 240)
                work.pairs(part, to - 1, first_pair, 16, pl.multiple_of(before - 688, 16))

            @pl.when((place < chain // 2) & (to == 3))
            def _():
                work.down(part, 672, 16, pl.multiple_of(before - 128, 16), 128)

            trade(to)
            return carry

        lax.fori_loop(0, chain, group, 0)

    last_row = 4 * step_rows + HEAD_ROWS

    @pl.when(section == WINDOW)
    def _():
        work.start_attention()
        for index in range(3):
            work.window(part, index)
        trade(0)
        work.window(part, 3)
        done = HEAD_ROWS + 4 * 8192
        clear(part, done, last_row - done)
        trade(1)

    @pl.when(section == LINEAR)
    def _():
        work.start_attention()
        work.linear(part)
        done = HEAD_ROWS + 20480
        clear(part, done, last_row - done)
        trade(0)
        trade(1)

    def pass_on(t, carry):
        upward, downward = ends - 1 - t, t

        def step(i):
            @pl.when((place > 0) & (upward > place))
            def _():
                slot = up_slot(place, upward)
                rows = rows_of(i)
                arrived(slot, i)
                added = passing[slot, rows, :].astype(F32) + own[upward, rows, :].astype(F32)
                passing[slot, rows, :] = added.astype(BF)
                go_up(passing.at[slot, rows, :], upward, i).start()

            @pl.when((place < chain - 1) & (downward < place))
            def _():
                slot = down_slot(place, downward)
                rows = rows_of(i)
                arrived(slot, i)
                added = passing[slot, rows, :].astype(F32) + own[downward, rows, :].astype(F32)
                passing[slot, rows, :] = added.astype(BF)
                go_down(passing.at[slot, rows, :], downward, i).start()

        each_chunk(step)
        return carry

    lax.fori_loop(0, ends, pass_on, 0)

    def finish(i):
        rows = rows_of(i)

        @pl.when(place < ends)
        def _():
            total[...] = own[place, rows, :].astype(F32)

        @pl.when(place >= ends)
        def _():
            total[...] = jnp.zeros_like(total)

        @pl.when((place > 0) & (place < ends))
        def _():
            arrived(0, i)
            total[...] += passing[0, rows, :].astype(F32)

        @pl.when((place < chain - 1) & (place < ends))
        def _():
            arrived(chain, i)
            total[...] += passing[chain, rows, :].astype(F32)

        flat[0:1, pl.ds(pl.multiple_of(i * piece * 128, 1024), piece * 128)] = total[...].reshape(1, piece * 128)

    each_chunk(finish)
    count = out.shape[1]
    first = pl.multiple_of((8 + batch) * 128, 128)
    store = pltpu.make_async_copy(flat.at[:, pl.ds(first, count)], out, out_sem)
    store.start()

    def drain(t, carry):
        upward, downward = ends - 1 - t, t

        def step(i):
            @pl.when((place < chain - 1) & (upward > place))
            def _():
                go_up(passing.at[0, rows_of(i), :], upward, i).wait_send()

            @pl.when((place > 0) & (downward < place))
            def _():
                go_down(passing.at[0, rows_of(i), :], downward, i).wait_send()

        each_chunk(step)
        return carry

    lax.fori_loop(0, ends, drain, 0)
    store.wait()


def reduce_products(sources, total_rows, batches):
    chain = batches // 2
    step_rows = (total_rows - 8) // batches - 1
    width = step_rows + HEAD_ROWS
    return pl.pallas_call(
        functools.partial(reduce_kernel, chain),
        out_shape=jax.ShapeDtypeStruct((1, (step_rows + 1) * 128), F32),
        in_specs=[any_spec()] * 5 + [vmem_spec()],
        out_specs=any_spec(),
        scratch_shapes=[
            pltpu.VMEM((total_rows, 128), BF),
            pltpu.VMEM((chain, width, 128), BF),
            pltpu.VMEM((chain + 1, width, 128), BF),
            pltpu.VMEM((width // CHUNKS, 128), F32),
            pltpu.VMEM((1, width * 128), F32),
            (
                pltpu.SemaphoreType.DMA((chain,)),
                pltpu.SemaphoreType.DMA((chain,)),
                pltpu.SemaphoreType.DMA((chain - 1, CHUNKS)),
                pltpu.SemaphoreType.DMA((chain - 1, CHUNKS)),
                pltpu.SemaphoreType.DMA((chain + 1, CHUNKS)),
                pltpu.SemaphoreType.DMA,
            ),
        ]
        + product_scratch(),
        compiler_params=pltpu.CompilerParams(
            collective_id=1, has_side_effects=True, vmem_limit_bytes=62 * MIB
        ),
        name="reduce_products",
    )(*sources)


def document_ids(lengths):
    ends = jnp.cumsum(lengths, axis=1)
    places = jnp.arange(LEN, dtype=jnp.int32)
    return jnp.sum((places[None, :, None] >= ends[:, None, :]).astype(jnp.int32), axis=2)


def shards(tokens, cotangent, params, lengths):
    docs = document_ids(lengths[0])
    doc_col, doc_row = docs[:, :, None], docs[:, None, :]
    acts, d_inputs, normed, middle, d_first, d_second, grads, d_gain = train(
        tokens, cotangent, params, doc_col, doc_row
    )
    total_rows = params.shape[1] // 128 + 8
    sources = (normed, d_first, d_second, middle, grads, d_gain)
    batches = lax.axis_size("batch")
    if batches == 8:
        mine = reduce_products(sources, total_rows, batches)
    else:
        parts = products(sources, total_rows)
        mine = lax.psum_scatter(parts[8:].reshape(-1), "batch", scatter_dimension=0, tiled=True)
        mine = mine.astype(F32)[None]
    return acts[None], d_inputs[None], mine


def solution(mesh):
    return jax.shard_map(
        shards,
        mesh=mesh,
        in_specs=(P("batch", None), P("batch", None), P("section", None), P("batch", None, None)),
        out_specs=(P("section", "batch", None), P("section", "batch", None), P("section", "batch")),
        check_vma=False,
    )
```

time: 455 us -> 323 us (0.71)
  Pallas kernels: 437 us -> 313 us
  local copies, waits for them, and re-layouts: 15.1 us -> 8.27 us
    pallas_call x3 -> x1, Pallas kernels: 238 us -> 114 us  [train(): pl.pallas_call(train_kernel, out_shape=(jax.ShapeDtypeStruct((count, D),...]
    unnamed x11 -> x7, local copies, waits for them, and re-layouts: 13.6 us -> 6.83 us
where the time goes in v3:
time: 323 us; the launch traced here: 322 us
  Pallas kernels  313 us (97%)
  local copies, waits for them, and re-layouts  8.27 us (3%)
    pallas_call x1, Pallas kernels, reduce_products(): pl.pallas_call(functools.partial(reduce_kernel, chain), out_shape=jax.Sha...  199 us
    pallas_call x1, Pallas kernels, train(): pl.pallas_call(train_kernel, out_shape=(jax.ShapeDtypeStruct((count, D),...  114 us
    unnamed x7, local copies, waits for them, and re-layouts  6.83 us

profile of v3, /device:TPU:10, one launch (start us, length us, event | category | flops | bytes accessed | tf_op | source)
XLA Modules:
  0.0 322.5 jit_solution(6446861128722058077)
XLA Ops:
  0.6 0.9 reduce_window_sum.14
  1.5 0.1 convert_reduce_fusion
  1.6 0.6 broadcast_in_dim.15.doc_row
  2.2 0.9 copy.8.doc_col
  3.0 113.9 %train.1 = (bf16[512,1024]{1,0:T(8,128)(2,1)}, f32[512,1024]{1,0:T(8,128)}, bf16[512,1024]{1,0:T(8,128)(2,1)}, bf16[512,2816]{1,0:T(8,128)(2,1)}, bf16[512,2816]...) custom-call(bf16[512,1024]{1,0:T(8,128)(2,1)} %tokens.1, ...), custom_call_target="tpu_custom_call" | custom-call | tf_op jit(solution)/shard_map/train/pallas_call | solution.py:526
  116.9 0.0 copy-start.1
  116.9 198.7 %reduce_products.1 = f32[1,1056896]{1,0:T(1,128)} custom-call(bf16[512,1024]{1,0:T(8,128)(2,1)} %get-tuple-element.13.refs_0_, bf16[512,2816]{1,0:T(8,128)(2,1)} %get-tuple-element.14.refs_1_, bf16[512,2816]{1,0:T(8,128)(2,1)} %get-tuple-element.15.refs_2_, bf16[512,2816]{1,0:T(8,128)(2,1)} %get-tuple-element.16.refs_3_, ...), custom_call_target="tpu_custom_call" | custom-call | tf_op jit(solution)/shard_map/reduce_products/pallas_call | solution.py:1045
  315.6 0.0 copy-done.1
  315.7 0.0 copy-start
  315.7 1.0 copy.12
  316.6 3.8 %copy.13 = f32[1,512,1024]{2,1,0:T(8,128)} copy(f32[1,512,1024]{2,1,0:T(8,128)} %bitcast.4) | data formatting | bytes 4194304
  320.5 0.0 copy-done
  320.5 2.0 copy.14
Async XLA Ops:
  116.9 198.7 %copy-start.1 = (bf16[512,1024]{1,0:T(8,128)(2,1)S(1)}, bf16[512,1024]{1,0:T(8,128)(2,1)}, u32[]{:S(2)}) copy-start(bf16[512,1024]{1,0:T(8,128)(2,1)} %get-tuple-element.11) | copy-start | bytes 3145732
  315.7 4.8 %copy-start = (f32[1,1056896]{1,0:T(1,128)S(1)}, f32[1,1056896]{1,0:T(1,128)}, u32[]{:S(2)}) copy-start(f32[1,1056896]{1,0:T(1,128)} %reduce_products.1) | copy-start | bytes 12682756
